TPU v7x, 128 devices: a whole 4x4x4 slice. The times are simulated.
128 devices in a mesh: seq: 32 (over z, y, core), head: 4 (over x).
Axes of the slice: x: 4, y: 4, z: 4, core: 2. Of those that a mesh axis runs over, the one named last changes fastest.
Arguments:
- hidden_in: bfloat16 [64, 8192], P(None, 'seq'), may hold values from -6 to 6
- w_query: bfloat16 [8192, 8192], P('seq', 'head'), may hold values from -0.0625 to 0.0625
- w_keyval: bfloat16 [8192, 2048], P('seq', 'head'), may hold values from -0.0625 to 0.0625
- w_out: bfloat16 [8192, 8192], P('head', 'seq'), may hold values from -0.0625 to 0.0625
- key_cache: bfloat16 [4096, 128, 1024], P('seq', None, 'head'), may hold values from -6 to 6
- value_cache: bfloat16 [4096, 128, 1024], P('seq', None, 'head'), may hold values from -6 to 6
- key_scale: float32 [4096, 8], P('seq', 'head'), may hold values from 0.25 to 300
- value_scale: float32 [4096, 8], P('seq', 'head'), may hold values from 0.5 to 2
- page_counts: int32 [64], replicated, may hold values from 1 to 512, 4096 in all
- slot_pages: int32 [4096], P('seq'), may hold values from 0 to 4095, each once
- trim: int32 [64], replicated, may hold values from 0 to 127
Outputs:
- attn_out: bfloat16 [64, 8192], P(None, 'seq')
Inputs may be any that keep to these rules, and one draw needn't show every extreme that they name: `page_counts`: every request has at least one page; the page counts sum to 4096.
All inputs are finite; a program needn't handle non-finite values.
Results may differ from a plain program's by a relative error of at most 0.0095.
Values may be sent and summed in bfloat16 or wider, within the bound.
A program may use at most 128 MiB of HBM per device.

v0:
```python
import math

import jax
import jax.numpy as jnp
from jax import lax
from jax.sharding import PartitionSpec as P

HD = 128
PAGE = 128


masked_low = -1e30


def widen(factor, size):
    return jnp.repeat(factor, size, axis=1)


def finish(query, keyval, cache_max, cache_sum, cache_out, kv_local, group):
    inverse_square_root = 1.0 / math.sqrt(HD)
    requests = query.shape[0]
    heads_local = kv_local * group
    pairs = keyval.reshape(requests, kv_local, 2, HD)
    new_key = pairs[:, :, 0]
    new_value = pairs[:, :, 1].astype(jnp.float32)
    query_heads = query.reshape(requests, kv_local, group, HD)
    own = (
        jnp.einsum(
            "rgjd,rgd->rgj", query_heads, new_key, preferred_element_type=jnp.float32
        ).reshape(requests, heads_local)
        * inverse_square_root
    )
    top = jnp.maximum(cache_max, own)
    old_part = jnp.exp(cache_max - top)
    new_part = jnp.exp(own - top)
    denom = cache_sum * old_part + new_part
    spread_value = jnp.broadcast_to(
        new_value[:, :, None, :], (requests, kv_local, group, HD)
    ).reshape(requests, heads_local * HD)
    numer = cache_out * widen(old_part, HD) + widen(new_part, HD) * spread_value
    return (numer / widen(denom, HD)).astype(jnp.bfloat16)


def body(
    hidden_in,
    w_query,
    w_keyval,
    w_out,
    key_cache,
    value_cache,
    key_scale,
    value_scale,
    page_counts,
    slot_pages,
    trim,
):
    requests = hidden_in.shape[0]
    slots = key_cache.shape[0]
    kv_local = w_keyval.shape[1] // (2 * HD)
    heads_local = w_query.shape[1] // HD
    group = heads_local // kv_local
    part_query = jnp.dot(hidden_in, w_query, preferred_element_type=jnp.float32)
    part_keyval = jnp.dot(hidden_in, w_keyval, preferred_element_type=jnp.float32)
    sum_query, sum_keyval = lax.psum((part_query, part_keyval), "seq")
    query = sum_query.astype(jnp.bfloat16)
    keyval = sum_keyval.astype(jnp.bfloat16)
    start = jnp.cumsum(page_counts) - page_counts
    ends = start + page_counts
    owner = jnp.sum((ends[None, :] <= slot_pages[:, None]).astype(jnp.int32), axis=1)
    selector = owner[:, None] == jnp.arange(requests, dtype=jnp.int32)[None, :]
    select_int = selector.astype(jnp.int32)
    index = slot_pages - jnp.sum(select_int * start[None, :], axis=1)
    lengths = PAGE * page_counts - trim
    page_len = jnp.sum(select_int * lengths[None, :], axis=1)
    inverse_square_root = 1.0 / math.sqrt(HD)
    q_sel = jnp.dot(
        selector.astype(jnp.bfloat16), query, preferred_element_type=jnp.float32
    ).astype(jnp.bfloat16)
    q_sel = q_sel.reshape(slots, kv_local, group, HD)
    key_rows = key_cache.reshape(slots, PAGE, kv_local, HD)
    value_rows = value_cache.reshape(slots, PAGE, kv_local, HD)
    unscaled_pages = jnp.einsum(
        "sgjd,stgd->sgjt", q_sel, key_rows, preferred_element_type=jnp.float32
    )
    score_matrix = unscaled_pages * (key_scale * inverse_square_root)[:, :, None, None]
    position = index[:, None] * PAGE + jnp.arange(PAGE, dtype=jnp.int32)[None, :]
    valid = (position < page_len[:, None])[:, None, None, :]
    score_matrix = jnp.where(valid, score_matrix, masked_low)
    page_max = jnp.max(score_matrix, axis=-1)
    probs = jnp.where(valid, jnp.exp(score_matrix - page_max[..., None]), 0.0).astype(jnp.bfloat16)
    page_sum = jnp.sum(probs.astype(jnp.float32), axis=-1).reshape(slots, heads_local)
    page_out = jnp.einsum("sgjt,stgd->sgjd", probs, value_rows, preferred_element_type=jnp.float32)
    page_out = (page_out * value_scale[:, :, None, None]).reshape(slots, heads_local, HD)
    page_max = page_max.reshape(slots, heads_local)
    select_float = selector.astype(jnp.float32)
    dev_max = jnp.max(jnp.where(selector[:, :, None], page_max[:, None, :], masked_low), axis=0)
    slot_max = jnp.max(jnp.where(selector[:, :, None], dev_max[None, :, :], masked_low), axis=1)
    weight = jnp.exp(page_max - slot_max)
    dev_sum = jnp.dot(select_float.T, page_sum * weight, precision=lax.Precision.HIGHEST)
    weighted = (page_out * weight[:, :, None]).reshape(slots, heads_local * HD)
    dev_out = jnp.dot(select_float.T, weighted, precision=lax.Precision.HIGHEST)
    cache_max = lax.pmax(dev_max, "seq")
    factor = jnp.exp(dev_max - cache_max)
    cache_sum, cache_out = lax.psum((dev_sum * factor, dev_out * widen(factor, HD)), "seq")
    context = finish(query, keyval, cache_max, cache_sum, cache_out, kv_local, group)
    partial_out = jnp.dot(context, w_out, preferred_element_type=jnp.float32)
    return lax.psum(partial_out, "head").astype(jnp.bfloat16)


def solution(mesh):
    return jax.shard_map(
        body,
        mesh=mesh,
        in_specs=(
            P(None, "seq"),
            P("seq", "head"),
            P("seq", "head"),
            P("head", "seq"),
            P("seq", None, "head"),
            P("seq", None, "head"),
            P("seq", "head"),
            P("seq", "head"),
            P(),
            P("seq"),
            P(),
        ),
        out_specs=P(None, "seq"),
        check_vma=False,
    )
```

profile of v0, /device:TPU:0, one launch (start us, length us, event | category | flops | bytes accessed | tf_op | source)
XLA Modules:
  0.0 387.1 jit_solution(11376297957845269164)
XLA Ops:
  6.5 0.8 copy.51
  7.6 0.8 convert_reduce_fusion.1
  8.3 0.7 multiply_subtract_fusion
  9.0 0.6 iota_compare_fusion
  9.7 0.7 subtract_multiply_fusion
  10.4 1.1 fusion.35
  11.4 134.2 %all-reduce.6 = bf16[64,2048]{1,0:T(8,128)(2,1)S(1)} all-reduce(f32[64,2048]{1,0:T(8,128)S(1)} %fusion.35), channel_id=1, replica_groups=mesh['seq'=32,'head'=4] {'seq'}, use_global_device_ids=true, to_apply=%region_4.5 | all-reduce | flops 131072 | bytes 786432 | tf_op jit(solution)/shard_map/psum | solution.py:64
  145.6 0.3 fusion.15
  146.1 0.7 broadcast_multiply_fusion
  147.0 7.0 %fusion.34 = (f32[128,2,8]{2,1,0:T(2,128)S(1)}, f32[128,2,8,128]{3,2,1,0:T(8,128)S(1)}) fusion(f32[128,2]{1,0:T(8,128)S(1)} %copy.53, bf16[128,2,8,128]{3,2,1,0:T(8,128)(2,1)S(1)} %bitcast.104, pred[128,128]{1,0:T(8,128)(4,1)S(1)} %add_compare_fusion, bf16[128,128,256]{2,1,0:T(8,128)(2,1)} %param.15), kind=kOutput, calls=%fused_computation.54 | convolution fusion | flops 67893248 | bytes 9987072 | tf_op jit(solution)/shard_map/sgjd,stgd->sgjt/dot_general | solution.py:82
  154.7 63.7 %pmax.7 = f32[64,16]{0,1:T(8,128)S(1)} all-reduce(f32[64,16]{0,1:T(8,128)S(1)} %copy.59), channel_id=1, replica_groups=mesh['seq'=32,'head'=4] {'seq'}, use_global_device_ids=true, to_apply=%region_8.9 | all-reduce | flops 1024 | bytes 8192 | tf_op jit(solution)/shard_map/pmax | solution.py:102
  218.4 0.6 copy-done.6
  219.0 0.7 copy.60
  219.7 0.7 copy.57
  220.5 4.8 %fusion.9 = f32[128,2,8,128]{3,2,1,0:T(8,128)S(1)} fusion(f32[128,2]{1,0:T(8,128)S(1)} %copy.55, f32[128,2,8,128]{3,2,1,0:T(8,128)S(1)} %get-tuple-element.17, f32[128,2,8]{2,1,0:T(2,128)S(1)} %get-tuple-element.16, pred[128,128]{1,0:T(8,128)(4,1)S(1)} %add_compare_fusion, bf16[128,128,256]{2,1,0:T(8,128)(2,1)} %param.16), kind=kOutput, calls=%fused_computation.9 | convolution fusion | flops 68157440 | bytes 10511360 | tf_op jit(solution)/shard_map/sgjt,stgd->sgjd/dot_general | solution.py:92
  225.8 2.7 convolution_multiply_fusion
  228.5 1.4 convert_reduce_fusion
  229.9 1.0 copy.64
  230.9 0.9 convolution_multiply_fusion.1
  231.7 1.2 fusion.36
  232.9 125.3 %all-reduce.7 = (bf16[64,512]{1,0:T(8,128)(2,1)S(1)}, f32[64,16]{0,1:T(8,128)S(1)}) all-reduce(f32[64,512]{1,0:T(8,128)S(1)} %fusion.36, f32[64,16]{0,1:T(8,128)S(1)} %convolution_multiply_fusion.1), channel_id=1, replica_groups=mesh['seq'=32,'head'=4] {'seq'}, use_global_device_ids=true, to_apply=%region_10.11 | all-reduce | flops 33792 | bytes 204800 | tf_op jit(solution)/shard_map/psum | solution.py:64
  358.8 0.7 multiply_add_fusion
  360.4 1.8 fusion.21
  362.2 18.1 %psum.39 = bf16[64,256]{1,0:T(8,128)(2,1)} all-reduce(f32[64,256]{1,0:T(8,128)S(1)} %fusion.21), channel_id=1, replica_groups=mesh['seq'=32,'head'=4] {'head'}, use_global_device_ids=true, to_apply=%region_13.14 | all-reduce | flops 16384 | bytes 98304 | tf_op jit(solution)/shard_map/psum | solution.py:107
  (50 shorter events, 3.3 us)
Async XLA Ops:
  6.5 3.9 copy-start
  6.5 353.2 %all-reduce.5.cloned.1.call-start = ((), (), s32[]{:S(2)}) async-start(), calls=%async_computation | async-start | bytes 1048576 | tf_op jit(solution)/shard_map/psum | solution.py:104
  8.3 138.7 %copy-start.8 = (s32[128]{0:T(128)}, s32[128]{0:T(128)S(1)}, u32[]{:S(2)}) copy-start(s32[128]{0:T(128)S(1)} %convert_reduce_fusion.1) | copy-start | bytes 1540
  146.1 8.0 %copy-start.7 = (pred[128,64]{0,1:T(8,128)(4,1)S(1)}, pred[128,64]{0,1:T(8,128)(4,1)}, u32[]{:S(2)}) copy-start(pred[128,64]{0,1:T(8,128)(4,1)} %iota_compare_fusion) | copy-start | bytes 24580
  146.1 8.5 %copy-start.9 = (f32[128,2]{0,1:T(2,128)S(1)}, f32[128,2]{0,1:T(2,128)}, u32[]{:S(2)}) copy-start(f32[128,2]{0,1:T(2,128)} %param.18) | copy-start | bytes 3076
  218.4 0.6 copy-start.6
  219.0 1.4 copy-start.4
  219.7 0.7 copy-start.5
  220.4 4.8 %copy-start.3 = (f32[64,16]{1,0:T(8,128)S(1)}, f32[64,16]{1,0:T(8,128)}, u32[]{:S(2)}) copy-start(f32[64,16]{1,0:T(8,128)} %copy.60) | copy-start | bytes 12292
  220.4 5.0 %copy-start.2 = (f32[128,16]{1,0:T(8,128)S(1)}, f32[128,16]{1,0:T(8,128)}, u32[]{:S(2)}) copy-start(f32[128,16]{1,0:T(8,128)} %copy.57) | copy-start | bytes 24580
  225.2 135.2 %copy-start.1 = (bf16[2048,256]{1,0:T(8,128)(2,1)S(1)}, bf16[2048,256]{1,0:T(8,128)(2,1)}, u32[]{:S(2)}) copy-start(bf16[2048,256]{1,0:T(8,128)(2,1)} %param.14) | copy-start | bytes 3145732
Sparse Core Ops, SparseCore 0:
  228.6 100.1 all-reduce.4
where the time goes:
time: 388 us; the launch traced here: 387 us
  blocking collectives  341 us (88%)
  matrix products  19.9 us (5%)
  between operations  13.6 us (4%)
  other arithmetic  6.49 us (2%)
  local copies, waits for them, and re-layouts  5.81 us (1%)
    psum x2, blocking collectives, body(): sum_query, sum_keyval = lax.psum((part_query, part_keyval), 'seq')  260 us
    pmax x1, blocking collectives, body(): cache_max = lax.pmax(dev_max, 'seq')  63.7 us
    psum x1, blocking collectives, body(): return lax.psum(partial_out, 'head').astype(jnp.bfloat16)  18.1 us
  transfers between devices with their start and end apart: 1, of which 0 were waited for; matrix products, arithmetic and copies ran while one was open for 2% of the time, Pallas kernels for 0%

commit v1 on v0

v1 whole, which is shorter than its diff:
```python
import functools
import math

import jax
import jax.numpy as jnp
from jax import lax
from jax.experimental import pallas as pl
from jax.experimental.pallas import tpu as pltpu
from jax.sharding import PartitionSpec as P

HD = 128
PAGE = 128
MESH = pl.DeviceIdType.MESH
masked_low = -1e30
f32 = jnp.float32
bf16 = jnp.bfloat16
inverse_square_root = 1.0 / math.sqrt(HD)


def each(low, high, step, unroll=1):
    def run(k, carry):
        step(k)
        return carry

    lax.fori_loop(low, high, run, 0, unroll=unroll)


def project(hid, wq, wkv, part):
    x = hid[...]
    for h in range(0, 16, 2):
        y = jnp.dot(x, wq[:, h * HD : (h + 2) * HD], preferred_element_type=f32)
        for c in range(2):
            for j in range(2):
                part[c, h + j, 0:32] = y[32 * c : 32 * c + 32, HD * j : HD * j + HD]
    for b in range(0, 4, 2):
        y = jnp.dot(x, wkv[:, b * HD : (b + 2) * HD], preferred_element_type=f32)
        for c in range(2):
            for j in range(2):
                for rows in range(4):
                    at = 32 * c + 8 * rows
                    part[c, rows * 4 + b + j, 32:40] = y[at : at + 8, HD * j : HD * j + HD]


def iota(shape, axis):
    return lax.broadcasted_iota(jnp.int32, shape, axis)


def page_table(cnt, slt, trm, ksv, sel, selt, nv, ks0, ks1):
    zeros = jnp.zeros((1, 64), f32)
    count = jnp.concatenate([cnt[...].astype(f32), zeros], axis=1)
    trim = jnp.concatenate([trm[...].astype(f32), zeros], axis=1)
    i, j = iota((128, 128), 0), iota((128, 128), 1)
    count_col = jnp.sum(jnp.where(i == j, count, 0.0), axis=1, keepdims=True)
    end_col = jnp.sum(jnp.where(j <= i, count, 0.0), axis=1, keepdims=True)
    end = jnp.sum(jnp.where(i <= j, count_col, 0.0), axis=0, keepdims=True)
    start, start_col = end - count, end_col - count_col
    page = slt[...].astype(f32)
    page_col = jnp.sum(jnp.where(i == j, page, 0.0), axis=1, keepdims=True)
    mine = (start <= page_col) & (page_col < end)
    sel[...] = jnp.where(mine, 1.0, 0.0)
    selt[...] = jnp.where((start_col <= page) & (page < end_col), 1.0, 0.0)[:64].astype(bf16)
    left = PAGE * count - trim - PAGE * (page_col - start)
    valid = jnp.sum(jnp.where(mine, left, 0.0), axis=1, keepdims=True)
    nv[...] = jnp.broadcast_to(valid, (128, 128))
    ks0[...] = jnp.broadcast_to(ksv[:, 0:1] * inverse_square_root, (128, 128))
    ks1[...] = jnp.broadcast_to(ksv[:, 1:2] * inverse_square_root, (128, 128))


def select_query(qall, sel, qs):
    onehot = sel[:, 0:64].astype(bf16)
    for h in range(16):
        q = qall[2 * h : 2 * h + 2].reshape(64, HD)
        qs[h * 128 : (h + 1) * 128] = jnp.dot(onehot, q, preferred_element_type=f32)


def attend(slot, kc, vc, qs, nv, ks0, ks1, po, pm, ps):
    q = qs[pl.ds(slot, 16, stride=128), :]
    none = jnp.zeros((8, HD), f32)
    left = jnp.concatenate([q[0:8], none], axis=0).astype(bf16)
    right = jnp.concatenate([none, q[8:16]], axis=0).astype(bf16)
    query = jnp.concatenate([left, right], axis=1)
    score = lax.dot_general(query, kc[slot], (((1,), (1,)), ((), ())), preferred_element_type=f32)
    scale0 = jnp.broadcast_to(ks0[pl.ds(slot, 1), :], (8, PAGE))
    scale1 = jnp.broadcast_to(ks1[pl.ds(slot, 1), :], (8, PAGE))
    score = score * jnp.concatenate([scale0, scale1], axis=0)
    tokens = jnp.broadcast_to(nv[pl.ds(slot, 1), :], (16, PAGE))
    valid = iota((16, PAGE), 1).astype(f32) < tokens
    score = jnp.where(valid, score, masked_low)
    top = jnp.max(score, axis=1, keepdims=True)
    probs = jnp.where(valid, jnp.exp(score - top), 0.0).astype(bf16)
    total = jnp.sum(probs.astype(f32), axis=1, keepdims=True)
    out = jnp.dot(probs, vc[slot], preferred_element_type=f32)
    at = pl.ds(pl.multiple_of(slot * 16, 16), 16)
    po[at, :] = jnp.concatenate([out[0:8, 0:HD], out[8:16, HD : 2 * HD]], axis=0)
    pm[at, :] = jnp.broadcast_to(top, (16, HD))
    ps[at, :] = jnp.broadcast_to(total, (16, HD))


def three(x):
    a = x.astype(bf16).astype(f32)
    b = (x - a).astype(bf16).astype(f32)
    return a, b, x - a - b


def fold(h, sel, selt, vsv, po, pm, ps, msg):
    rows = pl.ds(h, 128, stride=16)
    mine = sel[...] > 0.5
    page_max = pm[rows, :]
    dev_max = jnp.max(jnp.where(mine, page_max, masked_low), axis=0, keepdims=True)
    slot_max = jnp.max(jnp.where(mine, dev_max, masked_low), axis=1, keepdims=True)
    weight = jnp.exp(page_max - slot_max)
    dev_sum = jnp.sum(jnp.where(mine, ps[rows, :] * weight, 0.0), axis=0, keepdims=True)
    g = h // 8
    weighted = (po[rows, :] * (weight * vsv[:, g : g + 1])).astype(bf16)
    dev_out = jnp.dot(selt[...], weighted, preferred_element_type=f32).astype(bf16)
    row = iota((16, 128), 0)
    stats = jnp.zeros((16, 128), f32)
    for at, part in enumerate(three(dev_max) + three(dev_sum)):
        stats = jnp.where(row == at, part, stats)
    stats = stats.astype(bf16)
    for c in range(2):
        msg[2 * h + c, 0:32] = dev_out[32 * c : 32 * c + 32]
        msg[2 * h + c, 32:48] = stats


def finish(chip, core, rmsg, qown, kvall, flat, turned):
    flat[...] = jnp.zeros((128, 128), f32)
    maxes, sums = [], []
    for i in range(32):
        stats = rmsg[i, 32:48].astype(f32)
        maxes.append(stats[0:1] + stats[1:2] + stats[2:3])
        sums.append(stats[3:4] + stats[4:5] + stats[5:6])
    maxes = jnp.concatenate(maxes, axis=0)
    sums = jnp.concatenate(sums, axis=0)
    cache_max = jnp.max(maxes, axis=0, keepdims=True)
    factors = jnp.exp(maxes - cache_max)
    flat[0:32] = factors
    flat[32:33] = cache_max
    flat[33:34] = jnp.sum(sums * factors, axis=0, keepdims=True)
    turned[...] = flat[...].T
    cols = turned[pl.ds(pl.multiple_of(core * 32, 32), 32), :]
    cache_out = jnp.zeros((32, HD), f32)
    for i in range(32):
        cache_out = cache_out + cols[:, i : i + 1] * rmsg[i, 0:32].astype(f32)
    cache_max, cache_sum = cols[:, 32:33], cols[:, 33:34]
    at = chip // 8 * 2
    new_key = jnp.concatenate([kvall[4 * r + at] for r in range(4)], axis=0)
    new_value = jnp.concatenate([kvall[4 * r + at + 1] for r in range(4)], axis=0)
    own = jnp.sum(qown[...].astype(f32) * new_key, axis=1, keepdims=True) * inverse_square_root
    top = jnp.maximum(cache_max, own)
    old_part = jnp.exp(cache_max - top)
    new_part = jnp.exp(own - top)
    denom = cache_sum * old_part + new_part
    return ((cache_out * old_part + new_part * new_value) / denom).astype(bf16)


def kernel(
    hidden_in, w_query, w_keyval, w_out, key_cache, value_cache, key_scale, value_scale, page_counts, slot_pages, trim,
    out_ref,
    hid, wq, wkv, wo, kc, vc, ksv, vsv, cnt, slt, trm,
    part, sib, rsb, qown, kvown, qall, kvall, qs, po, pm, ps, sel, selt, nv, ks0, ks1,
    msg, rmsg, flat, turned, ctx_own, ctx_all, xsend, xrecv,
    load_sem, sib_sem, rs_send, rs_recv, q_send, q_recv, kv_send, kv_recv, o_send, o_recv, c_send, c_recv, x_send, x_recv,
):
    me, col = lax.axis_index("seq"), lax.axis_index("head")
    chip, core = me // 2, lax.rem(me, 2)
    sibling = me + 1 - 2 * core

    barrier = pltpu.get_barrier_semaphore()

    def greet(k):
        pl.semaphore_signal(barrier, inc=1, device_id=(lax.rem(me + k, 32), col), device_id_type=MESH)

    def greet_column(k):
        pl.semaphore_signal(barrier, inc=1, device_id=(me, lax.rem(col + k, 4)), device_id_type=MESH)

    each(1, 32, greet)
    each(1, 4, greet_column)

    def load(k, source, target):
        copy = pltpu.make_async_copy(source, target, load_sem.at[k])
        copy.start()
        return copy

    first = [load(0, hidden_in, hid), load(1, w_query, wq), load(2, w_keyval, wkv)]
    small = [
        load(3, page_counts, cnt), load(4, slot_pages, slt), load(5, trim, trm),
        load(6, key_scale, ksv), load(7, value_scale, vsv),
    ]
    for copy in first:
        copy.wait()
    keys, values, outs = load(8, key_cache, kc), load(9, value_cache, vc), load(10, w_out, wo)
    project(hid, wq, wkv, part)

    def send(source, target, send_sem, recv_sem, device):
        return pltpu.make_async_remote_copy(
            source, target, send_sem, recv_sem, device_id=device, device_id_type=MESH
        )

    pl.semaphore_wait(barrier, 34)
    swap = send(part.at[1 - core], sib, sib_sem.at[0], sib_sem.at[1], (sibling, col))
    swap.start()
    for copy in small:
        copy.wait()
    page_table(cnt, slt, trm, ksv, sel, selt, nv, ks0, ks1)
    swap.wait()
    sib[...] += part[core]

    def reduce_copy(k, there):
        peer = lax.rem(chip + k, 16)
        return send(sib.at[peer], rsb.at[peer if there else chip], rs_send.at[k], rs_recv.at[peer if there else chip],
                    (2 * peer + core, col))

    each(1, 16, lambda k: reduce_copy(k, False).start())
    rsb[chip] = sib[chip]
    each(1, 16, lambda k: reduce_copy(k, True).wait_recv())
    total = rsb[0]
    for i in range(1, 16):
        total = total + rsb[i]
    qown[...] = total[0:32].astype(bf16)
    kvown[...] = total[32:40].astype(bf16).astype(f32)

    def query_copy(k, there):
        peer = lax.rem(me + k, 32)
        at = peer if there else me
        return send(qown, qall.at[at], q_send.at[k], q_recv.at[at], (peer, col))

    def keyval_copy(k, there):
        peer = lax.rem(chip + k, 16)
        at = peer if there else chip
        return send(kvown, kvall.at[at], kv_send.at[k], kv_recv.at[at], (2 * peer + core, col))

    each(1, 32, lambda k: query_copy(k, False).start())
    each(1, 16, lambda k: keyval_copy(k, False).start())
    qall[me] = qown[...]
    kvall[chip] = kvown[...]
    keys.wait()
    values.wait()
    each(1, 32, lambda k: query_copy(k, True).wait_recv())
    select_query(qall, sel, qs)

    def slots(k):
        for u in range(8):
            attend(k * 8 + u, kc, vc, qs, nv, ks0, ks1, po, pm, ps)

    each(0, 16, slots)
    for h in range(16):
        fold(h, sel, selt, vsv, po, pm, ps, msg)

    def out_copy(k, there):
        peer = lax.rem(me + k, 32)
        at = peer if there else me
        return send(msg.at[peer], rmsg.at[at], o_send.at[k], o_recv.at[at], (peer, col))

    each(1, 32, lambda k: out_copy(k, False).start())
    rmsg[me] = msg[me]
    each(1, 16, lambda k: keyval_copy(k, True).wait_recv())
    each(1, 32, lambda k: out_copy(k, True).wait_recv())
    ctx_own[...] = finish(chip, core, rmsg, qown, kvall, flat, turned)

    def context_copy(k, there):
        peer = lax.rem(me + k, 32)
        at = peer if there else me
        return send(ctx_own, ctx_all.at[at], c_send.at[k], c_recv.at[at], (peer, col))

    each(1, 32, lambda k: context_copy(k, False).start())
    ctx_all[me] = ctx_own[...]
    outs.wait()
    each(1, 32, lambda k: context_copy(k, True).wait_recv())
    context = jnp.concatenate([ctx_all[2 * h : 2 * h + 2].reshape(64, HD) for h in range(16)], axis=1)
    result = jnp.dot(context, wo[...], preferred_element_type=f32)
    xsend[...] = result.astype(bf16)

    def head_copy(k, there):
        peer = lax.rem(col + k, 4)
        at = peer if there else col
        return send(xsend, xrecv.at[at], x_send.at[k], x_recv.at[at], (me, peer))

    each(1, 4, lambda k: head_copy(k, False).start())
    each(1, 4, lambda k: head_copy(k, True).wait_recv())
    for k in range(1, 4):
        result = result + xrecv[lax.rem(col + k, 4)].astype(f32)
    out_ref[...] = result.astype(bf16)

    each(1, 16, lambda k: reduce_copy(k, True).wait_send())
    each(1, 16, lambda k: keyval_copy(k, True).wait_send())
    each(1, 32, lambda k: query_copy(k, True).wait_send())
    each(1, 32, lambda k: out_copy(k, True).wait_send())
    each(1, 32, lambda k: context_copy(k, True).wait_send())
    each(1, 4, lambda k: head_copy(k, True).wait_send())


def body(
    hidden_in, w_query, w_keyval, w_out, key_cache, value_cache, key_scale, value_scale, page_counts, slot_pages, trim
):
    vmem = pltpu.VMEM
    dma = pltpu.SemaphoreType.DMA
    return pl.pallas_call(
        kernel,
        out_shape=jax.ShapeDtypeStruct((64, 256), bf16),
        in_specs=[pl.BlockSpec(memory_space=pl.ANY)] * 11,
        out_specs=pl.BlockSpec(memory_space=pltpu.VMEM),
        scratch_shapes=[
            vmem((64, 256), bf16), vmem((256, 2048), bf16), vmem((256, 512), bf16), vmem((2048, 256), bf16),
            vmem((128, PAGE, 256), bf16), vmem((128, PAGE, 256), bf16), vmem((128, 2), f32), vmem((128, 2), f32),
            vmem((1, 64), jnp.int32), vmem((1, 128), jnp.int32), vmem((1, 64), jnp.int32),
            vmem((2, 16, 40, HD), f32), vmem((16, 40, HD), f32), vmem((16, 40, HD), f32),
            vmem((32, HD), bf16), vmem((8, HD), f32), vmem((32, 32, HD), bf16), vmem((16, 8, HD), f32),
            vmem((2048, HD), f32), vmem((2048, HD), f32), vmem((2048, HD), f32), vmem((2048, HD), f32),
            vmem((128, 128), f32), vmem((64, 128), bf16), vmem((128, 128), f32),
            vmem((128, 128), f32), vmem((128, 128), f32),
            vmem((32, 48, HD), bf16), vmem((32, 48, HD), bf16), vmem((128, 128), f32), vmem((128, 128), f32),
            vmem((32, HD), bf16), vmem((32, 32, HD), bf16), vmem((64, 256), bf16), vmem((4, 64, 256), bf16),
            dma((11,)), dma((2,)), dma((16,)), dma((16,)), dma((32,)), dma((32,)), dma((16,)), dma((16,)),
            dma((32,)), dma((32,)), dma((32,)), dma((32,)), dma((4,)), dma((4,)),
        ],
        compiler_params=pltpu.CompilerParams(collective_id=0, has_side_effects=True, vmem_limit_bytes=40 << 20),
        cost_estimate=pl.CostEstimate(flops=300_000_000, bytes_accessed=20_000_000, transcendentals=300_000),
    )(
        hidden_in, w_query, w_keyval, w_out, key_cache, value_cache, key_scale, value_scale,
        page_counts.reshape(1, 64), slot_pages.reshape(1, 128), trim.reshape(1, 64),
    )


def solution(mesh):
    return jax.shard_map(
        body,
        mesh=mesh,
        in_specs=(
            P(None, "seq"),
            P("seq", "head"),
            P("seq", "head"),
            P("head", "seq"),
            P("seq", None, "head"),
            P("seq", None, "head"),
            P("seq", "head"),
            P("seq", "head"),
            P(),
            P("seq"),
            P(),
        ),
        out_specs=P(None, "seq"),
        check_vma=False,
    )
```

time: 388 us -> 90.6 us (0.23)
  the two profiles are of different devices: /device:TPU:0 before, /device:TPU:1 now
where the time goes in v1:
time: 90.6 us; the launch traced here: 90.2 us
  Pallas kernels  78.5 us (87%)
  local copies, waits for them, and re-layouts  11.7 us (13%)
    pallas_call x1, Pallas kernels, body(): pl.pallas_call(kernel, out_shape=jax.ShapeDtypeStruct((64, 256), bf16), i...  78.5 us
    unnamed x19, local copies, waits for them, and re-layouts  11.7 us

profile of v1, /device:TPU:1, one launch (start us, length us, event | category | flops | bytes accessed | tf_op | source)
XLA Modules:
  0.0 90.2 jit_solution(6862702950743418914)
XLA Ops:
  0.0 0.8 copy.12.key_scale
  0.8 0.8 copy.13.value_scale
  1.6 0.0 copy-start
  1.6 3.4 %copy-done = bf16[128,128,256]{2,1,0:T(8,128)(2,1)S(1)} copy-done((bf16[128,128,256]{2,1,0:T(8,128)(2,1)S(1)}, bf16[128,128,256]{2,1,0:T(8,128)(2,1)}, u32[]{:S(2)}) %copy-start) | copy-done | bytes 8388632
  5.0 0.0 copy-start.1
  5.0 1.2 %copy-done.1 = bf16[256,2048]{1,0:T(8,128)(2,1)S(1)} copy-done((bf16[256,2048]{1,0:T(8,128)(2,1)S(1)}, bf16[256,2048]{1,0:T(8,128)(2,1)}, u32[]{:S(2)}) %copy-start.1) | copy-done | bytes 1048600
  6.2 0.0 copy-start.2
  6.2 1.2 %copy-done.2 = bf16[2048,256]{1,0:T(8,128)(2,1)S(1)} copy-done((bf16[2048,256]{1,0:T(8,128)(2,1)S(1)}, bf16[2048,256]{1,0:T(8,128)(2,1)}, u32[]{:S(2)}) %copy-start.2) | copy-done | bytes 1048600
  7.4 0.0 copy-start.3
  7.4 0.9 %copy-done.3 = bf16[256,512]{1,0:T(8,128)(2,1)S(1)} copy-done((bf16[256,512]{1,0:T(8,128)(2,1)S(1)}, bf16[256,512]{1,0:T(8,128)(2,1)}, u32[]{:S(2)}) %copy-start.3) | copy-done | bytes 262168
  8.4 0.0 copy-start.4
  8.4 0.8 copy-done.4
  9.1 0.0 copy-start.5
  9.1 0.7 copy-done.5
  9.8 0.0 copy-start.6
  9.8 0.7 copy-done.6
  10.4 0.0 copy-start.7
  10.4 0.7 copy-done.7
  11.1 78.5 %shard_map.109 = bf16[64,256]{1,0:T(8,128)(2,1)S(1)} custom-call(bf16[64,256]{1,0:T(8,128)(2,1)S(1)} %copy-done.4, bf16[256,2048]{1,0:T(8,128)(2,1)S(1)} %copy-done.1, bf16[256,512]{1,0:T(8,128)(2,1)S(1)} %copy-done.3, bf16[2048,256]{1,0:T(8,128)(2,1)S(1)} %copy-done.2, bf16[128,128,256]{2,1,0:T(8,128)(2,1)S(1)} %copy-done, ...), custom_call_target="tpu_custom_call" | custom-call | flops 300000000 | bytes 20000000 | tf_op jit(solution)/shard_map/pallas_call | solution.py:298
  89.6 0.6 copy.15
Async XLA Ops:
  1.6 3.4 %copy-start = (bf16[128,128,256]{2,1,0:T(8,128)(2,1)S(1)}, bf16[128,128,256]{2,1,0:T(8,128)(2,1)}, u32[]{:S(2)}) copy-start(bf16[128,128,256]{2,1,0:T(8,128)(2,1)} %key_cache.1) | copy-start | bytes 25165828
  5.0 1.2 %copy-start.1 = (bf16[256,2048]{1,0:T(8,128)(2,1)S(1)}, bf16[256,2048]{1,0:T(8,128)(2,1)}, u32[]{:S(2)}) copy-start(bf16[256,2048]{1,0:T(8,128)(2,1)} %w_query.1) | copy-start | bytes 3145732
  6.2 1.2 %copy-start.2 = (bf16[2048,256]{1,0:T(8,128)(2,1)S(1)}, bf16[2048,256]{1,0:T(8,128)(2,1)}, u32[]{:S(2)}) copy-start(bf16[2048,256]{1,0:T(8,128)(2,1)} %w_out.1) | copy-start | bytes 3145732
  7.4 0.9 %copy-start.3 = (bf16[256,512]{1,0:T(8,128)(2,1)S(1)}, bf16[256,512]{1,0:T(8,128)(2,1)}, u32[]{:S(2)}) copy-start(bf16[256,512]{1,0:T(8,128)(2,1)} %w_keyval.1) | copy-start | bytes 786436
  8.4 0.8 copy-start.4
  9.1 0.7 copy-start.5
  9.8 0.7 copy-start.6
  10.4 0.7 copy-start.7

commit v2 on v1

--- a/solution.py
+++ b/solution.py
@@ -45,7 +45,7 @@
     return lax.broadcasted_iota(jnp.int32, shape, axis)
 
 
-def page_table(cnt, slt, trm, ksv, sel, selt, nv, ks0, ks1):
+def page_table(cnt, slt, trm, ksv, vsv, sel, selt, nv, ks0, ks1, vs):
     zeros = jnp.zeros((1, 64), f32)
     count = jnp.concatenate([cnt[...].astype(f32), zeros], axis=1)
     trim = jnp.concatenate([trm[...].astype(f32), zeros], axis=1)
@@ -55,15 +55,21 @@
     end = jnp.sum(jnp.where(i <= j, count_col, 0.0), axis=0, keepdims=True)
     start, start_col = end - count, end_col - count_col
     page = slt[...].astype(f32)
-    page_col = jnp.sum(jnp.where(i == j, page, 0.0), axis=1, keepdims=True)
+
+    def column(row):
+        return jnp.sum(jnp.where(i == j, row, 0.0), axis=1, keepdims=True)
+
+    page_col = column(page)
     mine = (start <= page_col) & (page_col < end)
     sel[...] = jnp.where(mine, 1.0, 0.0)
     selt[...] = jnp.where((start_col <= page) & (page < end_col), 1.0, 0.0)[:64].astype(bf16)
     left = PAGE * count - trim - PAGE * (page_col - start)
     valid = jnp.sum(jnp.where(mine, left, 0.0), axis=1, keepdims=True)
     nv[...] = jnp.broadcast_to(valid, (128, 128))
-    ks0[...] = jnp.broadcast_to(ksv[:, 0:1] * inverse_square_root, (128, 128))
-    ks1[...] = jnp.broadcast_to(ksv[:, 1:2] * inverse_square_root, (128, 128))
+    ks0[...] = jnp.broadcast_to(column(ksv[0:1, :]) * inverse_square_root, (128, 128))
+    ks1[...] = jnp.broadcast_to(column(ksv[1:2, :]) * inverse_square_root, (128, 128))
+    for g in range(2):
+        vs[g] = jnp.broadcast_to(column(vsv[g : g + 1, :]), (128, 128))
 
 
 def select_query(qall, sel, qs):
@@ -73,27 +79,34 @@
         qs[h * 128 : (h + 1) * 128] = jnp.dot(onehot, q, preferred_element_type=f32)
 
 
-def attend(slot, kc, vc, qs, nv, ks0, ks1, po, pm, ps):
-    q = qs[pl.ds(slot, 16, stride=128), :]
+def attend(slots, kc, vc, qs, nv, ks0, ks1, po, pm, ps):
     none = jnp.zeros((8, HD), f32)
-    left = jnp.concatenate([q[0:8], none], axis=0).astype(bf16)
-    right = jnp.concatenate([none, q[8:16]], axis=0).astype(bf16)
-    query = jnp.concatenate([left, right], axis=1)
-    score = lax.dot_general(query, kc[slot], (((1,), (1,)), ((), ())), preferred_element_type=f32)
-    scale0 = jnp.broadcast_to(ks0[pl.ds(slot, 1), :], (8, PAGE))
-    scale1 = jnp.broadcast_to(ks1[pl.ds(slot, 1), :], (8, PAGE))
-    score = score * jnp.concatenate([scale0, scale1], axis=0)
-    tokens = jnp.broadcast_to(nv[pl.ds(slot, 1), :], (16, PAGE))
-    valid = iota((16, PAGE), 1).astype(f32) < tokens
-    score = jnp.where(valid, score, masked_low)
-    top = jnp.max(score, axis=1, keepdims=True)
-    probs = jnp.where(valid, jnp.exp(score - top), 0.0).astype(bf16)
-    total = jnp.sum(probs.astype(f32), axis=1, keepdims=True)
-    out = jnp.dot(probs, vc[slot], preferred_element_type=f32)
-    at = pl.ds(pl.multiple_of(slot * 16, 16), 16)
-    po[at, :] = jnp.concatenate([out[0:8, 0:HD], out[8:16, HD : 2 * HD]], axis=0)
-    pm[at, :] = jnp.broadcast_to(top, (16, HD))
-    ps[at, :] = jnp.broadcast_to(total, (16, HD))
+    token = iota((16, PAGE), 1).astype(f32)
+    scores, valids = [], []
+    for slot in slots:
+        q = qs[pl.ds(slot, 16, stride=128), :]
+        left = jnp.concatenate([q[0:8], none], axis=0).astype(bf16)
+        right = jnp.concatenate([none, q[8:16]], axis=0).astype(bf16)
+        query = jnp.concatenate([left, right], axis=1)
+        score = lax.dot_general(query, kc[slot], (((1,), (1,)), ((), ())), preferred_element_type=f32)
+        scale0 = jnp.broadcast_to(ks0[pl.ds(slot, 1), :], (8, PAGE))
+        scale1 = jnp.broadcast_to(ks1[pl.ds(slot, 1), :], (8, PAGE))
+        score = score * jnp.concatenate([scale0, scale1], axis=0)
+        valid = token < jnp.broadcast_to(nv[pl.ds(slot, 1), :], (16, PAGE))
+        scores.append(jnp.where(valid, score, masked_low))
+        valids.append(valid)
+    tops = [jnp.max(score, axis=1, keepdims=True) for score in scores]
+    probs = [
+        jnp.where(valid, jnp.exp(score - top), 0.0).astype(bf16)
+        for score, valid, top in zip(scores, valids, tops)
+    ]
+    totals = [jnp.sum(prob.astype(f32), axis=1, keepdims=True) for prob in probs]
+    outs = [jnp.dot(prob, vc[slot], preferred_element_type=f32) for slot, prob in zip(slots, probs)]
+    for slot, out, top, total in zip(slots, outs, tops, totals):
+        at = pl.ds(pl.multiple_of(slot * 16, 16), 16)
+        po[at, :] = jnp.concatenate([out[0:8, 0:HD], out[8:16, HD : 2 * HD]], axis=0)
+        pm[at, :] = jnp.broadcast_to(top, (16, HD))
+        ps[at, :] = jnp.broadcast_to(total, (16, HD))
 
 
 def three(x):
@@ -102,7 +115,7 @@
     return a, b, x - a - b
 
 
-def fold(h, sel, selt, vsv, po, pm, ps, msg):
+def fold(h, sel, selt, vs, po, pm, ps, msg):
     rows = pl.ds(h, 128, stride=16)
     mine = sel[...] > 0.5
     page_max = pm[rows, :]
@@ -111,7 +124,7 @@
     weight = jnp.exp(page_max - slot_max)
     dev_sum = jnp.sum(jnp.where(mine, ps[rows, :] * weight, 0.0), axis=0, keepdims=True)
     g = h // 8
-    weighted = (po[rows, :] * (weight * vsv[:, g : g + 1])).astype(bf16)
+    weighted = (po[rows, :] * (weight * vs[g])).astype(bf16)
     dev_out = jnp.dot(selt[...], weighted, preferred_element_type=f32).astype(bf16)
     row = iota((16, 128), 0)
     stats = jnp.zeros((16, 128), f32)
@@ -158,7 +171,7 @@
     hidden_in, w_query, w_keyval, w_out, key_cache, value_cache, key_scale, value_scale, page_counts, slot_pages, trim,
     out_ref,
     hid, wq, wkv, wo, kc, vc, ksv, vsv, cnt, slt, trm,
-    part, sib, rsb, qown, kvown, qall, kvall, qs, po, pm, ps, sel, selt, nv, ks0, ks1,
+    part, sib, rsb, qown, kvown, qall, kvall, qs, po, pm, ps, sel, selt, nv, ks0, ks1, vs,
     msg, rmsg, flat, turned, ctx_own, ctx_all, xsend, xrecv,
     load_sem, sib_sem, rs_send, rs_recv, q_send, q_recv, kv_send, kv_recv, o_send, o_recv, c_send, c_recv, x_send, x_recv,
 ):
@@ -202,7 +215,7 @@
     swap.start()
     for copy in small:
         copy.wait()
-    page_table(cnt, slt, trm, ksv, sel, selt, nv, ks0, ks1)
+    page_table(cnt, slt, trm, ksv, vsv, sel, selt, nv, ks0, ks1, vs)
     swap.wait()
     sib[...] += part[core]
 
@@ -240,12 +253,11 @@
     select_query(qall, sel, qs)
 
     def slots(k):
-        for u in range(8):
-            attend(k * 8 + u, kc, vc, qs, nv, ks0, ks1, po, pm, ps)
-
-    each(0, 16, slots)
+        attend([k * 32 + u for u in range(32)], kc, vc, qs, nv, ks0, ks1, po, pm, ps)
+
+    each(0, 4, slots)
     for h in range(16):
-        fold(h, sel, selt, vsv, po, pm, ps, msg)
+        fold(h, sel, selt, vs, po, pm, ps, msg)
 
     def out_copy(k, there):
         peer = lax.rem(me + k, 32)
@@ -298,26 +310,26 @@
     return pl.pallas_call(
         kernel,
         out_shape=jax.ShapeDtypeStruct((64, 256), bf16),
-        in_specs=[pl.BlockSpec(memory_space=pl.ANY)] * 11,
+        in_specs=[pl.BlockSpec(memory_space=pltpu.HBM)] * 11,
         out_specs=pl.BlockSpec(memory_space=pltpu.VMEM),
         scratch_shapes=[
             vmem((64, 256), bf16), vmem((256, 2048), bf16), vmem((256, 512), bf16), vmem((2048, 256), bf16),
-            vmem((128, PAGE, 256), bf16), vmem((128, PAGE, 256), bf16), vmem((128, 2), f32), vmem((128, 2), f32),
+            vmem((128, PAGE, 256), bf16), vmem((128, PAGE, 256), bf16), vmem((2, 128), f32), vmem((2, 128), f32),
             vmem((1, 64), jnp.int32), vmem((1, 128), jnp.int32), vmem((1, 64), jnp.int32),
             vmem((2, 16, 40, HD), f32), vmem((16, 40, HD), f32), vmem((16, 40, HD), f32),
             vmem((32, HD), bf16), vmem((8, HD), f32), vmem((32, 32, HD), bf16), vmem((16, 8, HD), f32),
             vmem((2048, HD), f32), vmem((2048, HD), f32), vmem((2048, HD), f32), vmem((2048, HD), f32),
             vmem((128, 128), f32), vmem((64, 128), bf16), vmem((128, 128), f32),
-            vmem((128, 128), f32), vmem((128, 128), f32),
+            vmem((128, 128), f32), vmem((128, 128), f32), vmem((2, 128, 128), f32),
             vmem((32, 48, HD), bf16), vmem((32, 48, HD), bf16), vmem((128, 128), f32), vmem((128, 128), f32),
             vmem((32, HD), bf16), vmem((32, 32, HD), bf16), vmem((64, 256), bf16), vmem((4, 64, 256), bf16),
             dma((11,)), dma((2,)), dma((16,)), dma((16,)), dma((32,)), dma((32,)), dma((16,)), dma((16,)),
             dma((32,)), dma((32,)), dma((32,)), dma((32,)), dma((4,)), dma((4,)),
         ],
-        compiler_params=pltpu.CompilerParams(collective_id=0, has_side_effects=True, vmem_limit_bytes=40 << 20),
+        compiler_params=pltpu.CompilerParams(collective_id=0, has_side_effects=True, vmem_limit_bytes=63 << 20),
         cost_estimate=pl.CostEstimate(flops=300_000_000, bytes_accessed=20_000_000, transcendentals=300_000),
     )(
-        hidden_in, w_query, w_keyval, w_out, key_cache, value_cache, key_scale, value_scale,
+        hidden_in, w_query, w_keyval, w_out, key_cache, value_cache, key_scale.T, value_scale.T,
         page_counts.reshape(1, 64), slot_pages.reshape(1, 128), trim.reshape(1, 64),
     )
 

time: 90.6 us -> 52.4 us (0.58)
  Pallas kernels: 78.5 us -> 50.8 us
  local copies, waits for them, and re-layouts: 11.7 us -> 1.38 us
    pallas_call x1, Pallas kernels: 78.5 us -> 50.8 us  [body(): pl.pallas_call(kernel, out_shape=jax.ShapeDtypeStruct((64, 256), bf16), i...]
    unnamed x19 -> x1, local copies, waits for them, and re-layouts: 11.7 us -> 1.38 us
where the time goes in v2:
time: 52.4 us; the launch traced here: 52.2 us
  Pallas kernels  50.8 us (97%)
  local copies, waits for them, and re-layouts  1.38 us (3%)
    pallas_call x1, Pallas kernels, body(): pl.pallas_call(kernel, out_shape=jax.ShapeDtypeStruct((64, 256), bf16), i...  50.8 us
    unnamed x1, local copies, waits for them, and re-layouts  1.38 us

profile of v2, /device:TPU:1, one launch (start us, length us, event | category | flops | bytes accessed | tf_op | source)
XLA Modules:
  0.0 52.2 jit_solution(12877736176585057148)
XLA Ops:
  0.0 50.8 %shard_map.109 = bf16[64,256]{1,0:T(8,128)(2,1)} custom-call(bf16[64,256]{1,0:T(8,128)(2,1)} %hidden_in.1, bf16[256,2048]{1,0:T(8,128)(2,1)} %w_query.1, bf16[256,512]{1,0:T(8,128)(2,1)} %w_keyval.1, bf16[2048,256]{1,0:T(8,128)(2,1)} %w_out.1, bf16[128,128,256]{2,1,0:T(8,128)(2,1)} %key_cache.1, bf16[128,128,256]{2,1,0:T(8,128)(2,1)} %value_cache.1, ...), custom_call_target="tpu_custom_call" | custom-call | flops 300000000 | bytes 20000000 | tf_op jit(solution)/shard_map/pallas_call | solution.py:310
  50.8 1.4 %copy.13 = bf16[64,256]{1,0:T(8,128)(2,1)} copy(bf16[64,256]{1,0:T(8,128)(2,1)} %shard_map.109) | data formatting | bytes 65536

commit v3 on v2

v3 whole, which is shorter than its diff:
```python
import functools
import math

import jax
import jax.numpy as jnp
from jax import lax
from jax.experimental import pallas as pl
from jax.experimental.pallas import tpu as pltpu
from jax.sharding import PartitionSpec as P

HD = 128
PAGE = 128
MESH = pl.DeviceIdType.MESH
masked_low = -1e30
f32 = jnp.float32
bf16 = jnp.bfloat16
inverse_square_root = 1.0 / math.sqrt(HD)


distance = (0, 1, 2, 1)
AROUND = sorted(
    ((z, y) for z in range(4) for y in range(4) if (z, y) != (0, 0)), key=lambda step: -distance[step[0]] - distance[step[1]]
)
COLUMN = (2, 1, 3)


def step_by(chip, step, back=False):
    z, y = ((4 - step[0]) % 4, (4 - step[1]) % 4) if back else step
    return lax.rem(chip // 4 + z, 4) * 4 + lax.rem(lax.rem(chip, 4) + y, 4)


def project(hid, wq, wkv, part, part_kv):
    x = hid[...]
    for h in range(0, 16, 2):
        y = jnp.dot(x, wq[:, h * HD : (h + 2) * HD], preferred_element_type=f32)
        for c in range(2):
            for j in range(2):
                part[c, h + j] = y[32 * c : 32 * c + 32, HD * j : HD * j + HD]
    for b in range(0, 4, 2):
        y = jnp.dot(x, wkv[:, b * HD : (b + 2) * HD], preferred_element_type=f32)
        for c in range(2):
            for j in range(2):
                for rows in range(4):
                    at = 32 * c + 8 * rows
                    part_kv[c, rows * 4 + b + j] = y[at : at + 8, HD * j : HD * j + HD]


def each(low, high, step):
    def run(k, carry):
        step(k)
        return carry

    lax.fori_loop(low, high, run, 0)


def iota(shape, axis):
    return lax.broadcasted_iota(jnp.int32, shape, axis)


def page_table(cnt, slt, trm, ksv, vsv, sel, selt, nv, ks0, ks1, vs):
    zeros = jnp.zeros((1, 64), f32)
    count = jnp.concatenate([cnt[...].astype(f32), zeros], axis=1)
    trim = jnp.concatenate([trm[...].astype(f32), zeros], axis=1)
    i, j = iota((128, 128), 0), iota((128, 128), 1)
    count_col = jnp.sum(jnp.where(i == j, count, 0.0), axis=1, keepdims=True)
    end_col = jnp.sum(jnp.where(j <= i, count, 0.0), axis=1, keepdims=True)
    end = jnp.sum(jnp.where(i <= j, count_col, 0.0), axis=0, keepdims=True)
    start, start_col = end - count, end_col - count_col
    page = slt[...].astype(f32)

    def column(row):
        return jnp.sum(jnp.where(i == j, row, 0.0), axis=1, keepdims=True)

    page_col = column(page)
    mine = (start <= page_col) & (page_col < end)
    sel[...] = jnp.where(mine, 1.0, 0.0)
    selt[...] = jnp.where((start_col <= page) & (page < end_col), 1.0, 0.0)[:64].astype(bf16)
    left = PAGE * count - trim - PAGE * (page_col - start)
    valid = jnp.sum(jnp.where(mine, left, 0.0), axis=1, keepdims=True)
    nv[...] = jnp.broadcast_to(valid, (128, 128))
    ks0[...] = jnp.broadcast_to(column(ksv[0:1, :]) * inverse_square_root, (128, 128))
    ks1[...] = jnp.broadcast_to(column(ksv[1:2, :]) * inverse_square_root, (128, 128))
    for g in range(2):
        vs[g] = jnp.broadcast_to(column(vsv[g : g + 1, :]), (128, 128))


def select_query(h, qall, sel, qs):
    q = qall[pl.ds(2 * h, 2)].reshape(64, HD)
    at = pl.ds(pl.multiple_of(h * 128, 128), 128)
    qs[at, :] = jnp.dot(sel[:, 0:64].astype(bf16), q, preferred_element_type=f32)


def attend(slots, kc, vc, qs, nv, ks0, ks1, po, pm, ps):
    none = jnp.zeros((8, HD), f32)
    token = iota((16, PAGE), 1).astype(f32)
    scores, valids = [], []
    for slot in slots:
        q = qs[pl.ds(slot, 16, stride=128), :]
        left = jnp.concatenate([q[0:8], none], axis=0).astype(bf16)
        right = jnp.concatenate([none, q[8:16]], axis=0).astype(bf16)
        query = jnp.concatenate([left, right], axis=1)
        score = lax.dot_general(query, kc[slot], (((1,), (1,)), ((), ())), preferred_element_type=f32)
        scale0 = jnp.broadcast_to(ks0[pl.ds(slot, 1), :], (8, PAGE))
        scale1 = jnp.broadcast_to(ks1[pl.ds(slot, 1), :], (8, PAGE))
        score = score * jnp.concatenate([scale0, scale1], axis=0)
        valid = token < jnp.broadcast_to(nv[pl.ds(slot, 1), :], (16, PAGE))
        scores.append(jnp.where(valid, score, masked_low))
        valids.append(valid)
    tops = [jnp.max(score, axis=1, keepdims=True) for score in scores]
    probs = [
        jnp.where(valid, jnp.exp(score - top), 0.0).astype(bf16)
        for score, valid, top in zip(scores, valids, tops)
    ]
    totals = [jnp.sum(prob.astype(f32), axis=1, keepdims=True) for prob in probs]
    outs = [jnp.dot(prob, vc[slot], preferred_element_type=f32) for slot, prob in zip(slots, probs)]
    for slot, out, top, total in zip(slots, outs, tops, totals):
        at = pl.ds(pl.multiple_of(slot * 16, 16), 16)
        po[at, :] = jnp.concatenate([out[0:8, 0:HD], out[8:16, HD : 2 * HD]], axis=0)
        pm[at, :] = jnp.broadcast_to(top, (16, HD))
        ps[at, :] = jnp.broadcast_to(total, (16, HD))


def fold(h, sel, selt, vs, po, pm, ps, msg, stats):
    rows = pl.ds(h, 128, stride=16)
    mine = sel[...] > 0.5
    page_max = pm[rows, :]
    dev_max = jnp.max(jnp.where(mine, page_max, masked_low), axis=0, keepdims=True)
    slot_max = jnp.max(jnp.where(mine, dev_max, masked_low), axis=1, keepdims=True)
    weight = jnp.exp(page_max - slot_max)
    dev_sum = jnp.sum(jnp.where(mine, ps[rows, :] * weight, 0.0), axis=0, keepdims=True)
    stats[h] = jnp.concatenate([dev_max[:, 0:64], dev_sum[:, 0:64]], axis=1)
    weighted = (po[rows, :] * (weight * vs[h // 8])).astype(bf16)
    dev_out = jnp.dot(selt[...], weighted, preferred_element_type=f32).astype(bf16)
    for c in range(2):
        msg[2 * h + c] = dev_out[32 * c : 32 * c + 32]


def own_score(chip, qown, kvall):
    at = chip // 8 * 2
    new_key = jnp.concatenate([kvall[4 * r + at] for r in range(4)], axis=0)
    new_value = jnp.concatenate([kvall[4 * r + at + 1] for r in range(4)], axis=0)
    own = jnp.sum(qown[...].astype(f32) * new_key, axis=1, keepdims=True) * inverse_square_root
    return own, new_value


def finish(core, rmsg, rstats, own, new_value, flat, turned):
    stats = rstats[...].reshape(32, 128)
    cache_max = jnp.max(stats, axis=0, keepdims=True)
    factors = jnp.exp(stats - cache_max)
    sums = jnp.concatenate([stats[:, 64:128], stats[:, 0:64]], axis=1)
    flat[...] = jnp.zeros((128, 128), f32)
    flat[0:32] = factors
    flat[32:33] = cache_max
    flat[33:34] = jnp.sum(sums * factors, axis=0, keepdims=True)
    turned[...] = flat[...].T
    cols = turned[pl.ds(pl.multiple_of(core * 32, 32), 32), :]
    cache_out = jnp.zeros((32, HD), f32)
    for i in range(32):
        cache_out = cache_out + cols[:, i : i + 1] * rmsg[i].astype(f32)
    cache_max, cache_sum = cols[:, 32:33], cols[:, 33:34]
    top = jnp.maximum(cache_max, own)
    old_part = jnp.exp(cache_max - top)
    new_part = jnp.exp(own - top)
    denom = cache_sum * old_part + new_part
    return ((cache_out * old_part + new_part * new_value) / denom).astype(bf16)


def kernel(
    hidden_in, w_query, w_keyval, w_out, key_cache, value_cache, key_scale, value_scale, page_counts, slot_pages, trim,
    out_ref,
    hid, wq, wkv, wo, kc, vc, ksv, vsv, cnt, slt, trm,
    part, sib, rsb, part_kv, sib_kv, rsb_kv, qown, kvown, qall, kvall, qs, po, pm, ps, sel, selt, nv, ks0, ks1, vs,
    msg, rmsg, stats, rstats, flat, turned, ctx_own, ctx_all, xsend, xrecv,
    load_sem, sib_sem, rs_send, rs_recv, rk_send, rk_recv, q_send, q_recv, kv_send, kv_recv,
    o_send, o_recv, s_send, s_recv, c_send, c_recv, x_send, x_recv,
):
    me, col = lax.axis_index("seq"), lax.axis_index("head")
    chip, core = me // 2, lax.rem(me, 2)
    other = 1 - core
    sibling = 2 * chip + other

    def load(k, source, target):
        copy = pltpu.make_async_copy(source, target, load_sem.at[k])
        copy.start()
        return copy

    first = [load(0, hidden_in, hid), load(1, w_query, wq), load(2, w_keyval, wkv)]

    barrier = pltpu.get_barrier_semaphore()

    def greet(seq, head):
        pl.semaphore_signal(barrier, inc=1, device_id=(seq, head), device_id_type=MESH)

    for step in AROUND:
        for c in range(2):
            greet(2 * step_by(chip, step) + c, col)
    for k in COLUMN:
        for c in range(2):
            greet(2 * chip + c, lax.rem(col + k, 4))
    greet(sibling, col)

    small = [
        load(3, page_counts, cnt), load(4, slot_pages, slt), load(5, trim, trm),
        load(6, key_scale, ksv), load(7, value_scale, vsv),
    ]
    for copy in first:
        copy.wait()
    keys, values, outs = load(8, key_cache, kc), load(9, value_cache, vc), load(10, w_out, wo.at[core])
    project(hid, wq, wkv, part, part_kv)

    def send(source, target, send_sem, recv_sem, seq, head=col):
        return pltpu.make_async_remote_copy(
            source, target, send_sem, recv_sem, device_id=(seq, head), device_id_type=MESH
        )

    pl.semaphore_wait(barrier, 37)
    swap = send(part.at[other], sib, sib_sem.at[0], sib_sem.at[1], sibling)
    swap_kv = send(part_kv.at[other], sib_kv, sib_sem.at[2], sib_sem.at[3], sibling)
    swap.start()
    swap_kv.start()
    for copy in small:
        copy.wait()
    page_table(cnt, slt, trm, ksv, vsv, sel, selt, nv, ks0, ks1, vs)
    swap.wait_recv()
    sib[...] += part[core]

    reduces = []
    for i, step in enumerate(AROUND):
        peer = step_by(chip, step)
        reduces.append(send(sib.at[peer], rsb.at[i], rs_send.at[i], rs_recv.at[i], 2 * peer + core))
        reduces[-1].start()
    swap_kv.wait_recv()
    sib_kv[...] += part_kv[core]
    reduces_kv = []
    for i, step in enumerate(AROUND):
        peer = step_by(chip, step)
        reduces_kv.append(send(sib_kv.at[peer], rsb_kv.at[i], rk_send.at[i], rk_recv.at[i], 2 * peer + core))
        reduces_kv[-1].start()
    total = sib[chip]
    for i in reversed(range(15)):
        reduces[i].wait_recv()
        total = total + rsb[i]
    qown[...] = total.astype(bf16)

    queries = []
    for i, step in enumerate(AROUND):
        for c in range(2):
            peer = 2 * step_by(chip, step) + (other if c else core)
            queries.append(send(qown, qall.at[me], q_send.at[2 * i + c], q_recv.at[2 * i + c], peer))
            queries[-1].start()
    queries.append(send(qown, qall.at[me], q_send.at[30], q_recv.at[30], sibling))
    queries[-1].start()
    qall[me] = qown[...]

    total = sib_kv[chip]
    for i in reversed(range(15)):
        reduces_kv[i].wait_recv()
        total = total + rsb_kv[i]
    kvown[...] = total.astype(bf16).astype(f32)
    keyvals = []
    for i, step in enumerate(AROUND):
        peer = 2 * step_by(chip, step) + core
        keyvals.append(send(kvown, kvall.at[chip], kv_send.at[i], kv_recv.at[i], peer))
        keyvals[-1].start()
    kvall[chip] = kvown[...]
    outs.wait()
    share = send(wo.at[core], wo.at[core], sib_sem.at[4], sib_sem.at[5], sibling)
    share.start()

    def query_from(i, c, source):
        return send(qown, qall.at[source], q_send.at[2 * i + c], q_recv.at[2 * i + c], source)

    query_from(15, 0, sibling).wait_recv()
    select_query(chip, qall, sel, qs)
    for i in reversed(range(15)):
        source = step_by(chip, AROUND[i], back=True)
        for c in range(2):
            query_from(i, c, 2 * source + (other if c else core)).wait_recv()
        select_query(source, qall, sel, qs)
    keys.wait()
    values.wait()

    def slots(k):
        attend([k * 32 + u for u in range(32)], kc, vc, qs, nv, ks0, ks1, po, pm, ps)

    each(0, 4, slots)

    sent = []
    for i in range(0, 15, 4):
        group = range(i, min(i + 4, 15))
        heads = {k: step_by(chip, AROUND[k]) for k in group}
        for k in group:
            fold(heads[k], sel, selt, vs, po, pm, ps, msg, stats)
        for k in group:
            for c in range(2):
                half = other if c else core
                at = 2 * k + c
                peer = 2 * heads[k] + half
                sent.append(send(msg.at[peer], rmsg.at[at], o_send.at[at], o_recv.at[at], peer))
                sent.append(send(stats.at[heads[k]], rstats.at[at], s_send.at[at], s_recv.at[at], peer))
                sent[-2].start()
                sent[-1].start()
    fold(chip, sel, selt, vs, po, pm, ps, msg, stats)
    sent.append(send(msg.at[sibling], rmsg.at[30], o_send.at[30], o_recv.at[30], sibling))
    sent.append(send(stats.at[chip], rstats.at[30], s_send.at[30], s_recv.at[30], sibling))
    sent[-2].start()
    sent[-1].start()
    rmsg[31] = msg[me]
    rstats[31] = stats[chip]
    for i in reversed(range(15)):
        source = step_by(chip, AROUND[i], back=True)
        send(kvown, kvall.at[source], kv_send.at[i], kv_recv.at[i], 2 * source + core).wait_recv()
    own, new_value = own_score(chip, qown, kvall)
    for copy in reversed(sent):
        copy.wait_recv()
    ctx_own[...] = finish(core, rmsg, rstats, own, new_value, flat, turned)

    contexts = []
    for i, step in enumerate(AROUND):
        peer = 2 * step_by(chip, step) + core
        contexts.append(send(ctx_own, ctx_all.at[chip], c_send.at[i], c_recv.at[i], peer))
        contexts[-1].start()
    share.wait_send()
    send(wo.at[core], wo.at[other], sib_sem.at[4], sib_sem.at[5], sibling).wait_recv()

    def project_out(h, context, result):
        rows = pl.ds(pl.multiple_of(h * HD, HD), HD)
        return [y + jnp.dot(context, wo[c, rows, :], preferred_element_type=f32) for c, y in enumerate(result)]

    result = project_out(chip, ctx_own[...], [jnp.zeros((32, 256), f32)] * 2)
    for i in reversed(range(15)):
        source = step_by(chip, AROUND[i], back=True)
        send(ctx_own, ctx_all.at[source], c_send.at[i], c_recv.at[i], 2 * source + core).wait_recv()
        result = project_out(source, ctx_all[source], result)
    for c in range(2):
        xsend[c] = result[c].astype(bf16)

    ends = []
    for k in COLUMN:
        for c in range(2):
            half = other if c else core
            at = 2 * k + c
            there = lax.rem(col + k, 4)
            ends.append(send(xsend.at[half], xrecv.at[core, col], x_send.at[at], x_recv.at[at], 2 * chip + half, there))
            ends[-1].start()
    ends.append(send(xsend.at[other], xrecv.at[core, col], x_send.at[1], x_recv.at[1], sibling))
    ends[-1].start()
    xrecv[core, col] = xsend[core]
    for k in range(4):
        source = lax.rem(col + 4 - k, 4)
        for c in range(2):
            if k or c:
                half = other if c else core
                at = 2 * k + c
                send(xsend.at[0], xrecv.at[half, source], x_send.at[at], x_recv.at[at], 2 * chip + half, source).wait_recv()
    for c in range(2):
        result = xrecv[c, 0].astype(f32)
        for k in range(1, 4):
            result = result + xrecv[c, k].astype(f32)
        out_ref[32 * c : 32 * c + 32] = result.astype(bf16)

    swap.wait_send()
    swap_kv.wait_send()
    for copy in reduces + reduces_kv + queries + keyvals + sent + contexts + ends:
        copy.wait_send()


def body(
    hidden_in, w_query, w_keyval, w_out, key_cache, value_cache, key_scale, value_scale, page_counts, slot_pages, trim
):
    vmem = pltpu.VMEM
    dma = pltpu.SemaphoreType.DMA
    return pl.pallas_call(
        kernel,
        out_shape=jax.ShapeDtypeStruct((64, 256), bf16),
        in_specs=[pl.BlockSpec(memory_space=pltpu.HBM)] * 11,
        out_specs=pl.BlockSpec(memory_space=pltpu.VMEM),
        scratch_shapes=[
            vmem((64, 256), bf16), vmem((256, 2048), bf16), vmem((256, 512), bf16), vmem((2, 2048, 256), bf16),
            vmem((128, PAGE, 256), bf16), vmem((128, PAGE, 256), bf16), vmem((2, 128), f32), vmem((2, 128), f32),
            vmem((1, 64), jnp.int32), vmem((1, 128), jnp.int32), vmem((1, 64), jnp.int32),
            vmem((2, 16, 32, HD), f32), vmem((16, 32, HD), f32), vmem((15, 32, HD), f32),
            vmem((2, 16, 8, HD), f32), vmem((16, 8, HD), f32), vmem((15, 8, HD), f32),
            vmem((32, HD), bf16), vmem((8, HD), f32), vmem((32, 32, HD), bf16), vmem((16, 8, HD), f32),
            vmem((2048, HD), f32), vmem((2048, HD), f32), vmem((2048, HD), f32), vmem((2048, HD), f32),
            vmem((128, 128), f32), vmem((64, 128), bf16), vmem((128, 128), f32),
            vmem((128, 128), f32), vmem((128, 128), f32), vmem((2, 128, 128), f32),
            vmem((32, 32, HD), bf16), vmem((32, 32, HD), bf16), vmem((16, 1, 128), f32), vmem((32, 1, 128), f32),
            vmem((128, 128), f32), vmem((128, 128), f32),
            vmem((32, HD), bf16), vmem((16, 32, HD), bf16), vmem((2, 32, 256), bf16), vmem((2, 4, 32, 256), bf16),
            dma((11,)), dma((6,)), dma((15,)), dma((15,)), dma((15,)), dma((15,)), dma((31,)), dma((31,)),
            dma((15,)), dma((15,)), dma((31,)), dma((31,)), dma((31,)), dma((31,)), dma((15,)), dma((15,)),
            dma((8,)), dma((8,)),
        ],
        compiler_params=pltpu.CompilerParams(collective_id=0, has_side_effects=True, vmem_limit_bytes=63 << 20),
        cost_estimate=pl.CostEstimate(flops=300_000_000, bytes_accessed=20_000_000, transcendentals=300_000),
    )(
        hidden_in, w_query, w_keyval, w_out, key_cache, value_cache, key_scale.T, value_scale.T,
        page_counts.reshape(1, 64), slot_pages.reshape(1, 128), trim.reshape(1, 64),
    )


def solution(mesh):
    return jax.shard_map(
        body,
        mesh=mesh,
        in_specs=(
            P(None, "seq"),
            P("seq", "head"),
            P("seq", "head"),
            P("head", "seq"),
            P("seq", None, "head"),
            P("seq", None, "head"),
            P("seq", "head"),
            P("seq", "head"),
            P(),
            P("seq"),
            P(),
        ),
        out_specs=P(None, "seq"),
        check_vma=False,
    )
```

time: 52.4 us -> 48.9 us (0.933)
  Pallas kernels: 50.8 us -> 47.3 us
    pallas_call x1, Pallas kernels: 50.8 us -> 47.3 us  [body(): pl.pallas_call(kernel, out_shape=jax.ShapeDtypeStruct((64, 256), bf16), i...]
where the time goes in v3:
time: 48.9 us; the launch traced here: 48.7 us
  Pallas kernels  47.3 us (97%)
  local copies, waits for them, and re-layouts  1.38 us (3%)
    pallas_call x1, Pallas kernels, body(): pl.pallas_call(kernel, out_shape=jax.ShapeDtypeStruct((64, 256), bf16), i...  47.3 us
    unnamed x1, local copies, waits for them, and re-layouts  1.38 us

profile of v3, /device:TPU:1, one launch (start us, length us, event | category | flops | bytes accessed | tf_op | source)
XLA Modules:
  0.0 48.7 jit_solution(6210709654083252395)
XLA Ops:
  0.0 47.3 %shard_map.109 = bf16[64,256]{1,0:T(8,128)(2,1)} custom-call(bf16[64,256]{1,0:T(8,128)(2,1)} %hidden_in.1, bf16[256,2048]{1,0:T(8,128)(2,1)} %w_query.1, bf16[256,512]{1,0:T(8,128)(2,1)} %w_keyval.1, bf16[2048,256]{1,0:T(8,128)(2,1)} %w_out.1, bf16[128,128,256]{2,1,0:T(8,128)(2,1)} %key_cache.1, bf16[128,128,256]{2,1,0:T(8,128)(2,1)} %value_cache.1, ...), custom_call_target="tpu_custom_call" | custom-call | flops 300000000 | bytes 20000000 | tf_op jit(solution)/shard_map/pallas_call | solution.py:373
  47.3 1.4 %copy.13 = bf16[64,256]{1,0:T(8,128)(2,1)} copy(bf16[64,256]{1,0:T(8,128)(2,1)} %shard_map.109) | data formatting | bytes 65536

commit v4 on v3

--- a/solution.py
+++ b/solution.py
@@ -22,6 +22,8 @@
     ((z, y) for z in range(4) for y in range(4) if (z, y) != (0, 0)), key=lambda step: -distance[step[0]] - distance[step[1]]
 )
 COLUMN = (2, 1, 3)
+GROUPS = (range(0, 5), range(5, 11), range(11, 15))
+GROUP = [g for g, chips in enumerate(GROUPS) for _ in chips]
 
 
 def step_by(chip, step, back=False):
@@ -171,8 +173,7 @@
     hid, wq, wkv, wo, kc, vc, ksv, vsv, cnt, slt, trm,
     part, sib, rsb, part_kv, sib_kv, rsb_kv, qown, kvown, qall, kvall, qs, po, pm, ps, sel, selt, nv, ks0, ks1, vs,
     msg, rmsg, stats, rstats, flat, turned, ctx_own, ctx_all, xsend, xrecv,
-    load_sem, sib_sem, rs_send, rs_recv, rk_send, rk_recv, q_send, q_recv, kv_send, kv_recv,
-    o_send, o_recv, s_send, s_recv, c_send, c_recv, x_send, x_recv,
+    load_sem, sib_sem, send_sem, rs_recv, q_recv, kv_recv, o_recv, c_recv, x_recv,
 ):
     me, col = lax.axis_index("seq"), lax.axis_index("head")
     chip, core = me // 2, lax.rem(me, 2)
@@ -224,59 +225,52 @@
     swap.wait_recv()
     sib[...] += part[core]
 
-    reduces = []
+    def landed(ref, semaphore):
+        send(ref, ref, semaphore, semaphore, sibling).wait_recv()
+
+    def left(ref, semaphore):
+        send(ref, ref, semaphore, semaphore, sibling).wait_send()
+
     for i, step in enumerate(AROUND):
         peer = step_by(chip, step)
-        reduces.append(send(sib.at[peer], rsb.at[i], rs_send.at[i], rs_recv.at[i], 2 * peer + core))
-        reduces[-1].start()
+        send(sib.at[peer], rsb.at[i], send_sem.at[0], rs_recv.at[GROUP[i]], 2 * peer + core).start()
     swap_kv.wait_recv()
     sib_kv[...] += part_kv[core]
-    reduces_kv = []
-    for i, step in enumerate(AROUND):
-        peer = step_by(chip, step)
-        reduces_kv.append(send(sib_kv.at[peer], rsb_kv.at[i], rk_send.at[i], rk_recv.at[i], 2 * peer + core))
-        reduces_kv[-1].start()
     total = sib[chip]
-    for i in reversed(range(15)):
-        reduces[i].wait_recv()
-        total = total + rsb[i]
+    for g in (2, 1, 0):
+        landed(rsb.at[pl.ds(GROUPS[g][0], len(GROUPS[g]))], rs_recv.at[g])
+        for i in GROUPS[g]:
+            total = total + rsb[i]
     qown[...] = total.astype(bf16)
 
-    queries = []
     for i, step in enumerate(AROUND):
         for c in range(2):
             peer = 2 * step_by(chip, step) + (other if c else core)
-            queries.append(send(qown, qall.at[me], q_send.at[2 * i + c], q_recv.at[2 * i + c], peer))
-            queries[-1].start()
-    queries.append(send(qown, qall.at[me], q_send.at[30], q_recv.at[30], sibling))
-    queries[-1].start()
+            send(qown, qall.at[me], send_sem.at[1], q_recv.at[GROUP[i]], peer).start()
+    send(qown, qall.at[me], send_sem.at[1], q_recv.at[2], sibling).start()
+    for i, step in enumerate(AROUND):
+        peer = step_by(chip, step)
+        send(sib_kv.at[peer], rsb_kv.at[i], send_sem.at[2], kv_recv.at[0], 2 * peer + core).start()
     qall[me] = qown[...]
-
-    total = sib_kv[chip]
-    for i in reversed(range(15)):
-        reduces_kv[i].wait_recv()
-        total = total + rsb_kv[i]
-    kvown[...] = total.astype(bf16).astype(f32)
-    keyvals = []
-    for i, step in enumerate(AROUND):
-        peer = 2 * step_by(chip, step) + core
-        keyvals.append(send(kvown, kvall.at[chip], kv_send.at[i], kv_recv.at[i], peer))
-        keyvals[-1].start()
-    kvall[chip] = kvown[...]
     outs.wait()
     share = send(wo.at[core], wo.at[core], sib_sem.at[4], sib_sem.at[5], sibling)
     share.start()
 
-    def query_from(i, c, source):
-        return send(qown, qall.at[source], q_send.at[2 * i + c], q_recv.at[2 * i + c], source)
-
-    query_from(15, 0, sibling).wait_recv()
-    select_query(chip, qall, sel, qs)
-    for i in reversed(range(15)):
-        source = step_by(chip, AROUND[i], back=True)
-        for c in range(2):
-            query_from(i, c, 2 * source + (other if c else core)).wait_recv()
-        select_query(source, qall, sel, qs)
+    for g in (2, 1, 0):
+        landed(qall.at[pl.ds(0, 2 * len(GROUPS[g]) + (g == 2))], q_recv.at[g])
+        if g == 2:
+            select_query(chip, qall, sel, qs)
+        for i in GROUPS[g]:
+            select_query(step_by(chip, AROUND[i], back=True), qall, sel, qs)
+    landed(rsb_kv, kv_recv.at[0])
+    total = sib_kv[chip]
+    for i in range(15):
+        total = total + rsb_kv[i]
+    kvown[...] = total.astype(bf16).astype(f32)
+    for i, step in enumerate(AROUND):
+        peer = 2 * step_by(chip, step) + core
+        send(kvown, kvall.at[chip], send_sem.at[3], kv_recv.at[1], peer).start()
+    kvall[chip] = kvown[...]
     keys.wait()
     values.wait()
 
@@ -285,7 +279,6 @@
 
     each(0, 4, slots)
 
-    sent = []
     for i in range(0, 15, 4):
         group = range(i, min(i + 4, 15))
         heads = {k: step_by(chip, AROUND[k]) for k in group}
@@ -293,76 +286,64 @@
             fold(heads[k], sel, selt, vs, po, pm, ps, msg, stats)
         for k in group:
             for c in range(2):
-                half = other if c else core
                 at = 2 * k + c
-                peer = 2 * heads[k] + half
-                sent.append(send(msg.at[peer], rmsg.at[at], o_send.at[at], o_recv.at[at], peer))
-                sent.append(send(stats.at[heads[k]], rstats.at[at], s_send.at[at], s_recv.at[at], peer))
-                sent[-2].start()
-                sent[-1].start()
+                peer = 2 * heads[k] + (other if c else core)
+                send(msg.at[peer], rmsg.at[at], send_sem.at[4], o_recv.at[0], peer).start()
+                send(stats.at[heads[k]], rstats.at[at], send_sem.at[5], o_recv.at[1], peer).start()
     fold(chip, sel, selt, vs, po, pm, ps, msg, stats)
-    sent.append(send(msg.at[sibling], rmsg.at[30], o_send.at[30], o_recv.at[30], sibling))
-    sent.append(send(stats.at[chip], rstats.at[30], s_send.at[30], s_recv.at[30], sibling))
-    sent[-2].start()
-    sent[-1].start()
+    send(msg.at[sibling], rmsg.at[30], send_sem.at[4], o_recv.at[0], sibling).start()
+    send(stats.at[chip], rstats.at[30], send_sem.at[5], o_recv.at[1], sibling).start()
     rmsg[31] = msg[me]
     rstats[31] = stats[chip]
-    for i in reversed(range(15)):
-        source = step_by(chip, AROUND[i], back=True)
-        send(kvown, kvall.at[source], kv_send.at[i], kv_recv.at[i], 2 * source + core).wait_recv()
+    landed(kvall.at[pl.ds(0, 15)], kv_recv.at[1])
     own, new_value = own_score(chip, qown, kvall)
-    for copy in reversed(sent):
-        copy.wait_recv()
+    landed(rstats.at[pl.ds(0, 31)], o_recv.at[1])
+    landed(rmsg.at[pl.ds(0, 31)], o_recv.at[0])
     ctx_own[...] = finish(core, rmsg, rstats, own, new_value, flat, turned)
 
-    contexts = []
     for i, step in enumerate(AROUND):
         peer = 2 * step_by(chip, step) + core
-        contexts.append(send(ctx_own, ctx_all.at[chip], c_send.at[i], c_recv.at[i], peer))
-        contexts[-1].start()
+        send(ctx_own, ctx_all.at[chip], send_sem.at[6], c_recv.at[GROUP[i]], peer).start()
     share.wait_send()
-    send(wo.at[core], wo.at[other], sib_sem.at[4], sib_sem.at[5], sibling).wait_recv()
+    landed(wo.at[other], sib_sem.at[5])
 
     def project_out(h, context, result):
         rows = pl.ds(pl.multiple_of(h * HD, HD), HD)
         return [y + jnp.dot(context, wo[c, rows, :], preferred_element_type=f32) for c, y in enumerate(result)]
 
     result = project_out(chip, ctx_own[...], [jnp.zeros((32, 256), f32)] * 2)
-    for i in reversed(range(15)):
-        source = step_by(chip, AROUND[i], back=True)
-        send(ctx_own, ctx_all.at[source], c_send.at[i], c_recv.at[i], 2 * source + core).wait_recv()
-        result = project_out(source, ctx_all[source], result)
+    for g in (2, 1, 0):
+        landed(ctx_all.at[pl.ds(0, len(GROUPS[g]))], c_recv.at[g])
+        for i in GROUPS[g]:
+            source = step_by(chip, AROUND[i], back=True)
+            result = project_out(source, ctx_all[source], result)
     for c in range(2):
         xsend[c] = result[c].astype(bf16)
 
-    ends = []
+    mine = 4 * core + col
     for k in COLUMN:
-        for c in range(2):
-            half = other if c else core
-            at = 2 * k + c
+        for half in (core, other):
             there = lax.rem(col + k, 4)
-            ends.append(send(xsend.at[half], xrecv.at[core, col], x_send.at[at], x_recv.at[at], 2 * chip + half, there))
-            ends[-1].start()
-    ends.append(send(xsend.at[other], xrecv.at[core, col], x_send.at[1], x_recv.at[1], sibling))
-    ends[-1].start()
-    xrecv[core, col] = xsend[core]
-    for k in range(4):
-        source = lax.rem(col + 4 - k, 4)
-        for c in range(2):
-            if k or c:
-                half = other if c else core
-                at = 2 * k + c
-                send(xsend.at[0], xrecv.at[half, source], x_send.at[at], x_recv.at[at], 2 * chip + half, source).wait_recv()
+            send(xsend.at[half], xrecv.at[mine], send_sem.at[7], x_recv.at[0], 2 * chip + half, there).start()
+    send(xsend.at[other], xrecv.at[mine], send_sem.at[7], x_recv.at[0], sibling).start()
+    xrecv[mine] = xsend[core]
+    landed(xrecv.at[pl.ds(0, 7)], x_recv.at[0])
     for c in range(2):
-        result = xrecv[c, 0].astype(f32)
+        result = xrecv[4 * c].astype(f32)
         for k in range(1, 4):
-            result = result + xrecv[c, k].astype(f32)
+            result = result + xrecv[4 * c + k].astype(f32)
         out_ref[32 * c : 32 * c + 32] = result.astype(bf16)
 
     swap.wait_send()
     swap_kv.wait_send()
-    for copy in reduces + reduces_kv + queries + keyvals + sent + contexts + ends:
-        copy.wait_send()
+    left(rsb, send_sem.at[0])
+    left(qall.at[pl.ds(0, 31)], send_sem.at[1])
+    left(rsb_kv, send_sem.at[2])
+    left(kvall.at[pl.ds(0, 15)], send_sem.at[3])
+    left(rmsg.at[pl.ds(0, 31)], send_sem.at[4])
+    left(rstats.at[pl.ds(0, 31)], send_sem.at[5])
+    left(ctx_all.at[pl.ds(0, 15)], send_sem.at[6])
+    left(xrecv.at[pl.ds(0, 7)], send_sem.at[7])
 
 
 def body(
@@ -387,10 +368,8 @@
             vmem((128, 128), f32), vmem((128, 128), f32), vmem((2, 128, 128), f32),
             vmem((32, 32, HD), bf16), vmem((32, 32, HD), bf16), vmem((16, 1, 128), f32), vmem((32, 1, 128), f32),
             vmem((128, 128), f32), vmem((128, 128), f32),
-            vmem((32, HD), bf16), vmem((16, 32, HD), bf16), vmem((2, 32, 256), bf16), vmem((2, 4, 32, 256), bf16),
-            dma((11,)), dma((6,)), dma((15,)), dma((15,)), dma((15,)), dma((15,)), dma((31,)), dma((31,)),
-            dma((15,)), dma((15,)), dma((31,)), dma((31,)), dma((31,)), dma((31,)), dma((15,)), dma((15,)),
-            dma((8,)), dma((8,)),
+            vmem((32, HD), bf16), vmem((16, 32, HD), bf16), vmem((2, 32, 256), bf16), vmem((8, 32, 256), bf16),
+            dma((11,)), dma((6,)), dma((8,)), dma((3,)), dma((3,)), dma((2,)), dma((2,)), dma((3,)), dma((1,)),
         ],
         compiler_params=pltpu.CompilerParams(collective_id=0, has_side_effects=True, vmem_limit_bytes=63 << 20),
         cost_estimate=pl.CostEstimate(flops=300_000_000, bytes_accessed=20_000_000, transcendentals=300_000),

time: 48.9 us -> 44.9 us (0.918)
  Pallas kernels: 47.3 us -> 43.3 us
    pallas_call x1, Pallas kernels: 47.3 us -> 43.3 us  [body(): pl.pallas_call(kernel, out_shape=jax.ShapeDtypeStruct((64, 256), bf16), i...]
where the time goes in v4:
time: 44.9 us; the launch traced here: 44.7 us
  Pallas kernels  43.3 us (96%)
  local copies, waits for them, and re-layouts  1.38 us (3%)
    pallas_call x1, Pallas kernels, body(): pl.pallas_call(kernel, out_shape=jax.ShapeDtypeStruct((64, 256), bf16), i...  43.3 us
    unnamed x1, local copies, waits for them, and re-layouts  1.38 us

profile of v4, /device:TPU:1, one launch (start us, length us, event | category | flops | bytes accessed | tf_op | source)
XLA Modules:
  0.0 44.7 jit_solution(1600339919725268979)
XLA Ops:
  0.0 43.3 %shard_map.109 = bf16[64,256]{1,0:T(8,128)(2,1)} custom-call(bf16[64,256]{1,0:T(8,128)(2,1)} %hidden_in.1, bf16[256,2048]{1,0:T(8,128)(2,1)} %w_query.1, bf16[256,512]{1,0:T(8,128)(2,1)} %w_keyval.1, bf16[2048,256]{1,0:T(8,128)(2,1)} %w_out.1, bf16[128,128,256]{2,1,0:T(8,128)(2,1)} %key_cache.1, bf16[128,128,256]{2,1,0:T(8,128)(2,1)} %value_cache.1, ...), custom_call_target="tpu_custom_call" | custom-call | flops 300000000 | bytes 20000000 | tf_op jit(solution)/shard_map/pallas_call | solution.py:354
  43.3 1.4 %copy.13 = bf16[64,256]{1,0:T(8,128)(2,1)} copy(bf16[64,256]{1,0:T(8,128)(2,1)} %shard_map.109) | data formatting | bytes 65536

commit v5 on v4

--- a/solution.py
+++ b/solution.py
@@ -173,7 +173,7 @@
     hid, wq, wkv, wo, kc, vc, ksv, vsv, cnt, slt, trm,
     part, sib, rsb, part_kv, sib_kv, rsb_kv, qown, kvown, qall, kvall, qs, po, pm, ps, sel, selt, nv, ks0, ks1, vs,
     msg, rmsg, stats, rstats, flat, turned, ctx_own, ctx_all, xsend, xrecv,
-    load_sem, sib_sem, send_sem, rs_recv, q_recv, kv_recv, o_recv, c_recv, x_recv,
+    load_sem, sib_sem, send_sem, rs_recv, q_recv, kv_recv, o_recv, c_recv, x_recv, ready,
 ):
     me, col = lax.axis_index("seq"), lax.axis_index("head")
     chip, core = me // 2, lax.rem(me, 2)
@@ -192,10 +192,14 @@
     def greet(seq, head):
         pl.semaphore_signal(barrier, inc=1, device_id=(seq, head), device_id_type=MESH)
 
-    for step in AROUND:
-        for c in range(2):
-            greet(2 * step_by(chip, step) + c, col)
+    row, line = chip // 4, lax.rem(chip, 4)
+
+    def along_z(k):
+        return 2 * (4 * lax.rem(row + k, 4) + line) + core
+
     for k in COLUMN:
+        greet(2 * (4 * row + lax.rem(line + k, 4)) + core, col)
+        greet(along_z(k), col)
         for c in range(2):
             greet(2 * chip + c, lax.rem(col + k, 4))
     greet(sibling, col)
@@ -214,7 +218,9 @@
             source, target, send_sem, recv_sem, device_id=(seq, head), device_id_type=MESH
         )
 
-    pl.semaphore_wait(barrier, 37)
+    pl.semaphore_wait(barrier, 13)
+    for k in COLUMN:
+        pl.semaphore_signal(ready, inc=1, device_id=(along_z(k), col), device_id_type=MESH)
     swap = send(part.at[other], sib, sib_sem.at[0], sib_sem.at[1], sibling)
     swap_kv = send(part_kv.at[other], sib_kv, sib_sem.at[2], sib_sem.at[3], sibling)
     swap.start()
@@ -224,6 +230,7 @@
     page_table(cnt, slt, trm, ksv, vsv, sel, selt, nv, ks0, ks1, vs)
     swap.wait_recv()
     sib[...] += part[core]
+    pl.semaphore_wait(ready, 3)
 
     def landed(ref, semaphore):
         send(ref, ref, semaphore, semaphore, sibling).wait_recv()
@@ -370,6 +377,7 @@
             vmem((128, 128), f32), vmem((128, 128), f32),
             vmem((32, HD), bf16), vmem((16, 32, HD), bf16), vmem((2, 32, 256), bf16), vmem((8, 32, 256), bf16),
             dma((11,)), dma((6,)), dma((8,)), dma((3,)), dma((3,)), dma((2,)), dma((2,)), dma((3,)), dma((1,)),
+            pltpu.SemaphoreType.REGULAR,
         ],
         compiler_params=pltpu.CompilerParams(collective_id=0, has_side_effects=True, vmem_limit_bytes=63 << 20),
         cost_estimate=pl.CostEstimate(flops=300_000_000, bytes_accessed=20_000_000, transcendentals=300_000),

time: 44.9 us -> 43.8 us (0.976)
  Pallas kernels: 43.3 us -> 42.2 us
    pallas_call x1, Pallas kernels: 43.3 us -> 42.2 us  [body(): pl.pallas_call(kernel, out_shape=jax.ShapeDtypeStruct((64, 256), bf16), i...]
where the time goes in v5:
time: 43.8 us; the launch traced here: 43.6 us
  Pallas kernels  42.2 us (96%)
  local copies, waits for them, and re-layouts  1.38 us (3%)
    pallas_call x1, Pallas kernels, body(): pl.pallas_call(kernel, out_shape=jax.ShapeDtypeStruct((64, 256), bf16), i...  42.2 us
    unnamed x1, local copies, waits for them, and re-layouts  1.38 us

profile of v5, /device:TPU:1, one launch (start us, length us, event | category | flops | bytes accessed | tf_op | source)
XLA Modules:
  0.0 43.6 jit_solution(15549548849122035742)
XLA Ops:
  0.0 42.2 %shard_map.109 = bf16[64,256]{1,0:T(8,128)(2,1)} custom-call(bf16[64,256]{1,0:T(8,128)(2,1)} %hidden_in.1, bf16[256,2048]{1,0:T(8,128)(2,1)} %w_query.1, bf16[256,512]{1,0:T(8,128)(2,1)} %w_keyval.1, bf16[2048,256]{1,0:T(8,128)(2,1)} %w_out.1, bf16[128,128,256]{2,1,0:T(8,128)(2,1)} %key_cache.1, bf16[128,128,256]{2,1,0:T(8,128)(2,1)} %value_cache.1, ...), custom_call_target="tpu_custom_call" | custom-call | flops 300000000 | bytes 20000000 | tf_op jit(solution)/shard_map/pallas_call | solution.py:361
  42.2 1.4 %copy.13 = bf16[64,256]{1,0:T(8,128)(2,1)} copy(bf16[64,256]{1,0:T(8,128)(2,1)} %shard_map.109) | data formatting | bytes 65536

commit v6 on v5

--- a/solution.py
+++ b/solution.py
@@ -47,14 +47,6 @@
                     part_kv[c, rows * 4 + b + j] = y[at : at + 8, HD * j : HD * j + HD]
 
 
-def each(low, high, step):
-    def run(k, carry):
-        step(k)
-        return carry
-
-    lax.fori_loop(low, high, run, 0)
-
-
 def iota(shape, axis):
     return lax.broadcasted_iota(jnp.int32, shape, axis)
 
@@ -92,16 +84,23 @@
     qs[at, :] = jnp.dot(sel[:, 0:64].astype(bf16), q, preferred_element_type=f32)
 
 
+def turn_keys(kc):
+    def some(k, carry):
+        for u in range(16):
+            slot = k * 16 + u
+            kc[slot] = jnp.concatenate([kc[slot, :, 0:HD].T, kc[slot, :, HD : 2 * HD].T], axis=1)
+        return carry
+
+    lax.fori_loop(0, 8, some, 0)
+
+
 def attend(slots, kc, vc, qs, nv, ks0, ks1, po, pm, ps):
-    none = jnp.zeros((8, HD), f32)
     token = iota((16, PAGE), 1).astype(f32)
     scores, valids = [], []
     for slot in slots:
-        q = qs[pl.ds(slot, 16, stride=128), :]
-        left = jnp.concatenate([q[0:8], none], axis=0).astype(bf16)
-        right = jnp.concatenate([none, q[8:16]], axis=0).astype(bf16)
-        query = jnp.concatenate([left, right], axis=1)
-        score = lax.dot_general(query, kc[slot], (((1,), (1,)), ((), ())), preferred_element_type=f32)
+        query = qs[pl.ds(slot, 16, stride=128), :].astype(bf16)
+        score = jnp.dot(query, kc[slot], preferred_element_type=f32)
+        score = jnp.concatenate([score[0:8, 0:PAGE], score[8:16, PAGE : 2 * PAGE]], axis=0)
         scale0 = jnp.broadcast_to(ks0[pl.ds(slot, 1), :], (8, PAGE))
         scale1 = jnp.broadcast_to(ks1[pl.ds(slot, 1), :], (8, PAGE))
         score = score * jnp.concatenate([scale0, scale1], axis=0)
@@ -116,7 +115,7 @@
     totals = [jnp.sum(prob.astype(f32), axis=1, keepdims=True) for prob in probs]
     outs = [jnp.dot(prob, vc[slot], preferred_element_type=f32) for slot, prob in zip(slots, probs)]
     for slot, out, top, total in zip(slots, outs, tops, totals):
-        at = pl.ds(pl.multiple_of(slot * 16, 16), 16)
+        at = slice(slot * 16, slot * 16 + 16)
         po[at, :] = jnp.concatenate([out[0:8, 0:HD], out[8:16, HD : 2 * HD]], axis=0)
         pm[at, :] = jnp.broadcast_to(top, (16, HD))
         ps[at, :] = jnp.broadcast_to(total, (16, HD))
@@ -230,7 +229,6 @@
     page_table(cnt, slt, trm, ksv, vsv, sel, selt, nv, ks0, ks1, vs)
     swap.wait_recv()
     sib[...] += part[core]
-    pl.semaphore_wait(ready, 3)
 
     def landed(ref, semaphore):
         send(ref, ref, semaphore, semaphore, sibling).wait_recv()
@@ -238,11 +236,17 @@
     def left(ref, semaphore):
         send(ref, ref, semaphore, semaphore, sibling).wait_send()
 
-    for i, step in enumerate(AROUND):
-        peer = step_by(chip, step)
+    def reduce_to(i):
+        peer = step_by(chip, AROUND[i])
         send(sib.at[peer], rsb.at[i], send_sem.at[0], rs_recv.at[GROUP[i]], 2 * peer + core).start()
+
+    pl.semaphore_wait(ready, 3)
+    for i in range(15):
+        reduce_to(i)
     swap_kv.wait_recv()
     sib_kv[...] += part_kv[core]
+    keys.wait()
+    turn_keys(kc)
     total = sib[chip]
     for g in (2, 1, 0):
         landed(rsb.at[pl.ds(GROUPS[g][0], len(GROUPS[g]))], rs_recv.at[g])
@@ -269,6 +273,9 @@
             select_query(chip, qall, sel, qs)
         for i in GROUPS[g]:
             select_query(step_by(chip, AROUND[i], back=True), qall, sel, qs)
+    values.wait()
+
+    attend(range(0, 64), kc, vc, qs, nv, ks0, ks1, po, pm, ps)
     landed(rsb_kv, kv_recv.at[0])
     total = sib_kv[chip]
     for i in range(15):
@@ -278,13 +285,7 @@
         peer = 2 * step_by(chip, step) + core
         send(kvown, kvall.at[chip], send_sem.at[3], kv_recv.at[1], peer).start()
     kvall[chip] = kvown[...]
-    keys.wait()
-    values.wait()
-
-    def slots(k):
-        attend([k * 32 + u for u in range(32)], kc, vc, qs, nv, ks0, ks1, po, pm, ps)
-
-    each(0, 4, slots)
+    attend(range(64, 128), kc, vc, qs, nv, ks0, ks1, po, pm, ps)
 
     for i in range(0, 15, 4):
         group = range(i, min(i + 4, 15))

time: 43.8 us -> 42.4 us (0.968)
  Pallas kernels: 42.2 us -> 40.8 us
    pallas_call x1, Pallas kernels: 42.2 us -> 40.8 us  [body(): pl.pallas_call(kernel, out_shape=jax.ShapeDtypeStruct((64, 256), bf16), i...]
where the time goes in v6:
time: 42.4 us; the launch traced here: 42.2 us
  Pallas kernels  40.8 us (96%)
  local copies, waits for them, and re-layouts  1.38 us (3%)
    pallas_call x1, Pallas kernels, body(): pl.pallas_call(kernel, out_shape=jax.ShapeDtypeStruct((64, 256), bf16), i...  40.8 us
    unnamed x1, local copies, waits for them, and re-layouts  1.38 us

profile of v6, /device:TPU:1, one launch (start us, length us, event | category | flops | bytes accessed | tf_op | source)
XLA Modules:
  0.0 42.2 jit_solution(14342726620516296813)
XLA Ops:
  0.0 40.8 %shard_map.109 = bf16[64,256]{1,0:T(8,128)(2,1)} custom-call(bf16[64,256]{1,0:T(8,128)(2,1)} %hidden_in.1, bf16[256,2048]{1,0:T(8,128)(2,1)} %w_query.1, bf16[256,512]{1,0:T(8,128)(2,1)} %w_keyval.1, bf16[2048,256]{1,0:T(8,128)(2,1)} %w_out.1, bf16[128,128,256]{2,1,0:T(8,128)(2,1)} %key_cache.1, bf16[128,128,256]{2,1,0:T(8,128)(2,1)} %value_cache.1, ...), custom_call_target="tpu_custom_call" | custom-call | flops 300000000 | bytes 20000000 | tf_op jit(solution)/shard_map/pallas_call | solution.py:362
  40.8 1.4 %copy.13 = bf16[64,256]{1,0:T(8,128)(2,1)} copy(bf16[64,256]{1,0:T(8,128)(2,1)} %shard_map.109) | data formatting | bytes 65536

commit v7 on v6

--- a/solution.py
+++ b/solution.py
@@ -287,8 +287,8 @@
     kvall[chip] = kvown[...]
     attend(range(64, 128), kc, vc, qs, nv, ks0, ks1, po, pm, ps)
 
-    for i in range(0, 15, 4):
-        group = range(i, min(i + 4, 15))
+    for i in range(0, 15, 2):
+        group = range(i, min(i + 2, 15))
         heads = {k: step_by(chip, AROUND[k]) for k in group}
         for k in group:
             fold(heads[k], sel, selt, vs, po, pm, ps, msg, stats)
@@ -315,24 +315,23 @@
     share.wait_send()
     landed(wo.at[other], sib_sem.at[5])
 
-    def project_out(h, context, result):
+    def project_half(c, h, context):
         rows = pl.ds(pl.multiple_of(h * HD, HD), HD)
-        return [y + jnp.dot(context, wo[c, rows, :], preferred_element_type=f32) for c, y in enumerate(result)]
-
-    result = project_out(chip, ctx_own[...], [jnp.zeros((32, 256), f32)] * 2)
+        return jnp.dot(context, wo[c, rows, :], preferred_element_type=f32)
+
+    sources = [step_by(chip, step, back=True) for step in AROUND]
+    result = [project_half(c, chip, ctx_own[...]) for c in range(2)]
+    mine = 4 * core + col
     for g in (2, 1, 0):
         landed(ctx_all.at[pl.ds(0, len(GROUPS[g]))], c_recv.at[g])
-        for i in GROUPS[g]:
-            source = step_by(chip, AROUND[i], back=True)
-            result = project_out(source, ctx_all[source], result)
-    for c in range(2):
-        xsend[c] = result[c].astype(bf16)
-
-    mine = 4 * core + col
-    for k in COLUMN:
-        for half in (core, other):
-            there = lax.rem(col + k, 4)
-            send(xsend.at[half], xrecv.at[mine], send_sem.at[7], x_recv.at[0], 2 * chip + half, there).start()
+        for c in range(2):
+            for i in GROUPS[g]:
+                result[c] = result[c] + project_half(c, sources[i], ctx_all[sources[i]])
+            if g == 0:
+                xsend[c] = result[c].astype(bf16)
+                for k in COLUMN:
+                    send(xsend.at[c], xrecv.at[mine], send_sem.at[7], x_recv.at[0], 2 * chip + c, lax.rem(col + k, 4)).start()
+
     send(xsend.at[other], xrecv.at[mine], send_sem.at[7], x_recv.at[0], sibling).start()
     xrecv[mine] = xsend[core]
     landed(xrecv.at[pl.ds(0, 7)], x_recv.at[0])

time: 42.4 us -> 42.4 us (level)
  no operation moved by 1% of the time
where the time goes in v7:
time: 42.4 us; the launch traced here: 42.2 us
  Pallas kernels  40.8 us (96%)
  local copies, waits for them, and re-layouts  1.38 us (3%)
    pallas_call x1, Pallas kernels, body(): pl.pallas_call(kernel, out_shape=jax.ShapeDtypeStruct((64, 256), bf16), i...  40.8 us
    unnamed x1, local copies, waits for them, and re-layouts  1.38 us

profile of v7, /device:TPU:1, one launch (start us, length us, event | category | flops | bytes accessed | tf_op | source)
XLA Modules:
  0.0 42.2 jit_solution(6226113718075179894)
XLA Ops:
  0.0 40.8 %shard_map.109 = bf16[64,256]{1,0:T(8,128)(2,1)} custom-call(bf16[64,256]{1,0:T(8,128)(2,1)} %hidden_in.1, bf16[256,2048]{1,0:T(8,128)(2,1)} %w_query.1, bf16[256,512]{1,0:T(8,128)(2,1)} %w_keyval.1, bf16[2048,256]{1,0:T(8,128)(2,1)} %w_out.1, bf16[128,128,256]{2,1,0:T(8,128)(2,1)} %key_cache.1, bf16[128,128,256]{2,1,0:T(8,128)(2,1)} %value_cache.1, ...), custom_call_target="tpu_custom_call" | custom-call | flops 300000000 | bytes 20000000 | tf_op jit(solution)/shard_map/pallas_call | solution.py:361
  40.8 1.4 %copy.13 = bf16[64,256]{1,0:T(8,128)(2,1)} copy(bf16[64,256]{1,0:T(8,128)(2,1)} %shard_map.109) | data formatting | bytes 65536
